TPU v7x, 128 devices: a whole 4x4x4 slice. The times are simulated.
128 devices in a mesh: shard: 4 (over y), context: 16 (over x, z), tensor: 2 (over core).
Axes of the slice: x: 4, y: 4, z: 4, core: 2. Of those that a mesh axis runs over, the one named last changes fastest.
Arguments:
- tokens: bfloat16 [4, 2560, 2560], P('shard', 'context'), may hold values from -6 to 6
- lengths: int32 [4], P('shard'), may hold values from 1024 to 2560, as said below
- attn_gain: bfloat16 [2560], P(('shard', 'context')), may hold values from 0.5 to 1.5
- w_query: bfloat16 [2560, 2560], P(('shard', 'context'), 'tensor'), may hold values from -0.25 to 0.25
- w_keyval: bfloat16 [2560, 512], P(('shard', 'context')), may hold values from -0.125 to 0.125
- w_output: bfloat16 [2560, 2560], P(('shard', 'context'), 'tensor'), may hold values from -0.625 to 0.625
- mlp_gain: bfloat16 [2560], P(('shard', 'context')), may hold values from 0.5 to 1.5
- w_gate: bfloat16 [2560, 7680], P(('shard', 'context'), 'tensor'), may hold values from -0.125 to 0.125
- w_up: bfloat16 [2560, 7680], P(('shard', 'context'), 'tensor'), may hold values from -0.125 to 0.125
- w_down: bfloat16 [2560, 7680], P(('shard', 'context'), 'tensor'), may hold values from -0.0625 to 0.0625
- cotangent: bfloat16 [4, 2560, 2560], P('shard', 'context'), may hold values from -6 to 6
Outputs:
- block_out: bfloat16 [4, 2560, 2560], P('shard', 'context')
- tokens_grad: bfloat16 [4, 2560, 2560], P('shard', 'context')
- attn_gain_grad: float32 [2560], P(('shard', 'context'))
- query_grad: float32 [2560, 2560], P(('shard', 'context'), 'tensor')
- keyval_grad: float32 [2560, 512], P(('shard', 'context'))
- output_grad: float32 [2560, 2560], P(('shard', 'context'), 'tensor')
- mlp_gain_grad: float32 [2560], P(('shard', 'context'))
- gate_grad: float32 [2560, 7680], P(('shard', 'context'), 'tensor')
- up_grad: float32 [2560, 7680], P(('shard', 'context'), 'tensor')
- down_grad: float32 [2560, 7680], P(('shard', 'context'), 'tensor')
Inputs may be any that keep to these rules, and one draw needn't show every extreme that they name: `lengths`: valid tokens fill the end of each slot; at least one of the 4 slots holds 2560 valid tokens.
All inputs are finite; a program needn't handle non-finite values.
Results may differ from a plain program's by a relative error of at most 0.02.
Values may be sent and summed in bfloat16 or wider, within the bound.
No kernel may reach another device: no remote copies, remote signals or barrier semaphores. Data moves between devices by JAX's collectives and lax.ppermute only.
A program may use at most 448 MiB of HBM per device.

v0:
```python
import functools

import jax
import jax.numpy as jnp
from jax import lax
from jax.experimental import pallas as pl
from jax.experimental.pallas import tpu as pltpu
from jax.sharding import Mesh
from jax.sharding import PartitionSpec as P

WINDOW = 2048
SHARD_CONTEXT = ("shard", "context_0", "context_1")
CONTEXT = ("context_0", "context_1")
PIECES = ("context_0", "context_1", "shard")
Y, X, Z, T = "shard", "context_0", "context_1", "tensor"
VMEM = pltpu.CompilerParams(vmem_limit_bytes=48 * 2**20)
ANYWHERE = pl.BlockSpec(memory_space=pl.ANY)
FREE = pl.CostEstimate(flops=0, bytes_accessed=0, transcendentals=0)

EPSILON = 1e-06
NEGATIVE_FILL = -1e30
BF = jnp.bfloat16
F32 = jnp.float32


def shift(x, axis, by):
    n = lax.axis_size(axis)
    return lax.ppermute(x, axis, [(i, (i + by) % n) for i in range(n)])


def exchange(blocks, axis):
    return lax.all_to_all(blocks, axis, 0, 0, tiled=True)


def nothing(*refs):
    pass


def after(x, *others):
    return pl.pallas_call(
        nothing,
        out_shape=jax.ShapeDtypeStruct(x.shape, x.dtype),
        in_specs=[ANYWHERE] * (1 + len(others)),
        out_specs=ANYWHERE,
        input_output_aliases={0: 0},
        compiler_params=VMEM,
        cost_estimate=FREE,
    )(x, *others)


def small_trip(x, *others):
    corner = x.reshape(-1, x.shape[-1])[:8, :128]
    return shift(after(corner, *others) if others else corner, T, 1)


def ring_blocks(x, axis):
    return [x, shift(x, axis, -1), shift(x, axis, 2), shift(x, axis, 1)]


def place_kernel(axis, sign, *refs):
    blocks, out = refs[:4], refs[-1]
    me = lax.axis_index(axis)
    for r, block in enumerate(blocks):
        out[lax.rem(me + (sign * r) % 4, 4)] = block[...]


def place(blocks, axis, *first, sign=1):
    whole = pl.BlockSpec(memory_space=pltpu.VMEM)
    return pl.pallas_call(
        functools.partial(place_kernel, axis, sign),
        out_shape=jax.ShapeDtypeStruct((4, *blocks[0].shape), blocks[0].dtype),
        in_specs=[whole] * 4 + [ANYWHERE] * len(first),
        out_specs=whole,
        compiler_params=VMEM,
        cost_estimate=FREE,
    )(*blocks, *first)


def gather_rows(mine, *first):
    own = place(ring_blocks(mine, Y), Y, *first).reshape(320, -1)
    return own, shift(own, T, 1)


def rows_kernel(count, *refs):
    lefts, rights, (far_ref, near_ref) = refs[:count], refs[count : 2 * count], refs[-2:]
    total = dot(lefts[0][...], rights[0][...], 1, 1)
    for left, right in zip(lefts[1:], rights[1:]):
        total = total + dot(left[...], right[...], 1, 1)
    near_ref[...] = total[:320].astype(BF)
    far_ref[...] = total[320:].astype(BF)


def row_products(lefts, weight, at, width, *first):
    rows, count, n = 512, len(lefts), weight.shape[0]
    half = jax.ShapeDtypeStruct((320, n), BF)
    return pl.pallas_call(
        functools.partial(rows_kernel, count),
        grid=(n // rows,),
        out_shape=(half, half),
        in_specs=[pl.BlockSpec((640, width), lambda i: (0, 0))] * count
        + [pl.BlockSpec((rows, width), lambda i, j=j: (i, at + j)) for j in range(count)]
        + [ANYWHERE] * len(first),
        out_specs=(pl.BlockSpec((320, rows), lambda i: (0, i)),) * 2,
        compiler_params=VMEM,
        cost_estimate=FREE,
    )(*lefts, *[weight] * count, *first)


def core_sum(far, near):
    return (near.astype(F32) + shift(far, T, 1).astype(F32)).astype(BF).reshape(4, 80, -1)


def own_and_received(parts, axis, dim):
    me = lax.axis_index(axis)
    own, *rest = [
        lax.dynamic_index_in_dim(parts, (me + r) % 4, dim, keepdims=False) for r in range(4)
    ]
    return [own] + [shift(rest[r - 1], axis, r) for r in (1, 3, 2)]


def sums_kernel(kinds, *refs):
    for i, out in enumerate(refs[4 * len(kinds) :]):
        total = refs[4 * i][...].astype(F32)
        for ref in refs[4 * i + 1 : 4 * i + 4]:
            total = total + ref[...].astype(F32)
        out[...] = total.astype(kinds[i])


def sums(groups, kinds):
    return pl.pallas_call(
        functools.partial(sums_kernel, kinds),
        out_shape=tuple(jax.ShapeDtypeStruct(g[0].shape, k) for g, k in zip(groups, kinds)),
        compiler_params=VMEM,
        cost_estimate=FREE,
    )(*[block for group in groups for block in group])


def outer_kernel(x_ref, g_ref, out_ref):
    out_ref[...] = dot(x_ref[...], g_ref[...], 0, 0).astype(BF).reshape(4, 160, g_ref.shape[1])


def outer(x, g):
    cols = g.shape[1]
    return pl.pallas_call(
        outer_kernel,
        grid=(4,),
        out_shape=jax.ShapeDtypeStruct((16, 160, cols), BF),
        in_specs=[
            pl.BlockSpec((640, 640), lambda i: (0, i)),
            pl.BlockSpec((640, cols), lambda i: (0, 0)),
        ],
        out_specs=pl.BlockSpec((4, 160, cols), lambda i: (i, 0, 0)),
        compiler_params=VMEM,
        cost_estimate=FREE,
    )(x, g)


def outer_output_kernel(own_ref, other_ref, ob_ref, out_ref):
    cols = ob_ref.shape[2]
    part = dot(own_ref[...], ob_ref[:, :80].reshape(320, cols), 0, 0)
    part = part + dot(other_ref[...], ob_ref[:, 80:].reshape(320, cols), 0, 0)
    out_ref[...] = part.reshape(16, 40, cols).astype(BF)


def outer_output(own, other, ob):
    cols = 640
    half = pl.BlockSpec((320, 640), lambda i: (0, 0))
    return pl.pallas_call(
        outer_output_kernel,
        grid=(2,),
        out_shape=jax.ShapeDtypeStruct((16, 40, 1280), BF),
        in_specs=[half, half, pl.BlockSpec((4, 160, cols), lambda i: (0, 0, i))],
        out_specs=pl.BlockSpec((16, 40, cols), lambda i: (0, 0, i)),
        compiler_params=VMEM,
        cost_estimate=FREE,
    )(own, other, ob)


def to_owners(sums):
    me = lax.axis_index(Y)
    rows = sums.reshape(4, -1, sums.shape[-1])
    got = []
    for r in range(4):
        block = lax.dynamic_index_in_dim(rows, (me + r) % 4, 0, keepdims=False)
        got.append(shift(block, Y, r) if r else block)
    return got


def by_half(blocks):
    cols = blocks.shape[2]
    return blocks.reshape(4, 2, 80, cols).swapaxes(0, 1).reshape(640, cols)


def columns_out(blocks):
    me = lax.axis_index(Y)
    got = []
    for r in range(4):
        block = lax.dynamic_index_in_dim(blocks, (me + r) % 4, 0, keepdims=False)
        got.append(shift(block, Y, r) if r else block)
    return by_half(place(got, Y, sign=-1))


def quarters(x):
    rows = x.shape[0]
    return x.reshape(rows, 4, -1).swapaxes(0, 1)


def pack_attention_kernel(q_ref, kv_ref, gains_ref, attn_ref):
    attn_ref[...] = jnp.zeros_like(attn_ref)
    for j in range(4):
        attn_ref[j, :40, :320] = q_ref[:, 320 * j : 320 * j + 320]
        attn_ref[j, :40, 320:] = kv_ref[:, 64 * j : 64 * j + 64]
        attn_ref[j, 40:48, :128] = gains_ref[...]


def pack_attention(w_query, keyval_half, gains):
    return pl.pallas_call(
        pack_attention_kernel,
        out_shape=jax.ShapeDtypeStruct((4, 48, 384), BF),
        compiler_params=VMEM,
        cost_estimate=FREE,
    )(w_query, keyval_half, gains)


def pack_mlp_kernel(gate_ref, up_ref, down_ref, mlp_ref):
    mlp_ref[...] = jnp.zeros_like(mlp_ref)
    for j in range(4):
        mlp_ref[j, :, :960] = gate_ref[:, 960 * j : 960 * j + 960]
        mlp_ref[j, :, 1024:1984] = up_ref[:, 960 * j : 960 * j + 960]
        mlp_ref[j, :, 2048:3008] = down_ref[:, 960 * j : 960 * j + 960]


def pack_mlp(w_gate, w_up, w_down):
    return pl.pallas_call(
        pack_mlp_kernel,
        out_shape=jax.ShapeDtypeStruct((4, 40, 3072), BF),
        compiler_params=VMEM,
        cost_estimate=FREE,
    )(w_gate, w_up, w_down)


def down_grad_kernel(y_ref, hidden_ref, *rest):
    rest[-1][...] = dot(y_ref[...], hidden_ref[...], 0, 0).astype(BF)


def down_grads(grads, hidden, *first):
    rows = 512
    return pl.pallas_call(
        down_grad_kernel,
        grid=(2560 // rows,),
        out_shape=jax.ShapeDtypeStruct((2560, 3072), BF),
        in_specs=[
            pl.BlockSpec((640, rows), lambda i: (0, i)),
            pl.BlockSpec((640, 1024), lambda i: (0, 0)),
        ]
        + [ANYWHERE] * len(first),
        out_specs=pl.BlockSpec((rows, 1024), lambda i: (i, 2)),
        compiler_params=VMEM,
        cost_estimate=FREE,
    )(grads, hidden, *first)


def gate_up_grad_kernel(x_ref, gate_ref, up_ref, *rest):
    out_ref = rest[-1]
    out_ref[:, :1024] = dot(x_ref[...], gate_ref[...], 0, 0).astype(BF)
    out_ref[:, 1024:] = dot(x_ref[...], up_ref[...], 0, 0).astype(BF)


def gate_up_grads(normed, gate, up, held, *first):
    rows = 512
    whole = pl.BlockSpec((640, 1024), lambda i: (0, 0))
    return pl.pallas_call(
        gate_up_grad_kernel,
        grid=(2560 // rows,),
        out_shape=jax.ShapeDtypeStruct((2560, 3072), BF),
        in_specs=[pl.BlockSpec((640, rows), lambda i: (0, i)), whole, whole]
        + [ANYWHERE] * (1 + len(first)),
        out_specs=pl.BlockSpec((rows, 2048), lambda i: (i, 0)),
        input_output_aliases={3: 0},
        compiler_params=VMEM,
        cost_estimate=FREE,
    )(normed, gate, up, held, *first)


def feed_forward_kernel(x_ref, y_ref, gate_ref, up_ref, down_ref, *rest):
    hidden_out, gate_out, up_out = rest[-3:]
    gate = dot(x_ref[...], gate_ref[...], 1, 0)
    up = dot(x_ref[...], up_ref[...], 1, 0)
    grad = dot(y_ref[...], down_ref[...], 1, 0)
    scale = 0.7978845608028654
    square = gate * gate
    bent = jnp.tanh(scale * gate * (1.0 + 0.044715 * square))
    share = 0.5 * (1.0 + bent)
    slope = share + 0.5 * gate * (1.0 - bent * bent) * scale * (1.0 + 0.134145 * square)
    active = gate * share
    hidden_out[...] = (active * up).astype(BF)
    gate_out[...] = (grad * up * slope).astype(BF)
    up_out[...] = (grad * active).astype(BF)


def feed_forward(x, y, w_mlp, *first):
    cols = 256
    steps = 1024 // cols
    part = jax.ShapeDtypeStruct((640, 1024), BF)
    whole = pl.BlockSpec((640, 2560), lambda j: (0, 0))
    out = pl.BlockSpec((640, cols), lambda j: (0, j))
    return pl.pallas_call(
        feed_forward_kernel,
        grid=(steps,),
        out_shape=(part, part, part),
        in_specs=[whole, whole]
        + [pl.BlockSpec((2560, cols), lambda j, k=k: (0, k * steps + j)) for k in range(3)]
        + [ANYWHERE] * len(first),
        out_specs=(out, out, out),
        compiler_params=VMEM,
        cost_estimate=FREE,
    )(x, y, w_mlp, w_mlp, w_mlp, *first)


def to_piece_order(x):
    rows = x.shape[0]
    return x.reshape(rows, 4, 16, 40).swapaxes(1, 2).reshape(rows, 2560)


def inverse_root(values):
    return lax.rsqrt(jnp.mean(values * values, axis=-1, keepdims=True) + EPSILON)


def norm_back(grad, values, inverse, gain):
    scaled = gain * grad
    return inverse * scaled - values * inverse**3 * jnp.mean(
        scaled * values, axis=-1, keepdims=True
    )


def angles(position, head_dim):
    quarter = head_dim // 4
    frequency = 10000.0 ** (-jnp.arange(quarter, dtype=F32) / quarter)
    phase_angle = position[:, None].astype(F32) * frequency[None, :]
    return (jnp.cos(phase_angle), jnp.sin(phase_angle))


def dot(a, b, da, db):
    return lax.dot_general(a, b, (((da,), (db,)), ((), ())), preferred_element_type=F32)


def feature_quarters_kernel(x_ref, out_ref):
    for j in range(4):
        for p in range(16):
            at = 40 * (4 * p + j)
            out_ref[j, :, 40 * p : 40 * p + 40] = x_ref[:, at : at + 40].astype(BF)


def feature_quarters(x):
    return pl.pallas_call(
        feature_quarters_kernel,
        out_shape=jax.ShapeDtypeStruct((4, 80, 640), BF),
        compiler_params=VMEM,
        cost_estimate=FREE,
    )(x)


def project_kernel(own_ref, other_ref, gain_ref, weight_ref, normed_ref, out_ref):
    x = jnp.concatenate([own_ref[0], other_ref[0]]).astype(F32)
    normed = (x * inverse_root(x) * gain_ref[...]).astype(BF)
    normed_ref[0] = normed[:80]
    normed_ref[1] = normed[80:]
    out_ref[0] = dot(normed, weight_ref[...], 1, 0).astype(BF)


def project(own, other, gain, weight):
    rows = pl.BlockSpec((1, 80, 2560), lambda i: (i, 0, 0))
    normed, out = pl.pallas_call(
        project_kernel,
        grid=(4,),
        out_shape=(
            jax.ShapeDtypeStruct((2, 320, 2560), BF),
            jax.ShapeDtypeStruct((4, 160, 384), BF),
        ),
        in_specs=[
            rows,
            rows,
            pl.BlockSpec((1, 2560), lambda i: (0, 0)),
            pl.BlockSpec((2560, 384), lambda i: (0, 0)),
        ],
        out_specs=(
            pl.BlockSpec((2, 80, 2560), lambda i: (0, i, 0)),
            pl.BlockSpec((1, 160, 384), lambda i: (i, 0, 0)),
        ),
        compiler_params=VMEM,
        cost_estimate=FREE,
    )(own, other, gain, weight)
    return normed.reshape(640, 2560), out


def owners_kernel(*refs):
    home, mlp = refs[:4], refs[4:8]
    output_home, query_ref, keyval_ref, gate_ref, up_ref, block_mine, block_other, rows_mine, rows_other = refs[8:17]
    query_out, keyval_out, output_out, gate_out, up_out, down_out, gain_out, block_out, rows_out = refs[17:26]
    held, held_mlp = refs[26:]
    me = lax.axis_index(Y)
    for r in range(4):
        held[lax.rem(me + 4 - r, 4)] = home[r][...]
        held_mlp[lax.rem(me + 4 - r, 4)] = mlp[r][...]
    for j in range(4):
        columns = slice(960 * j, 960 * j + 960)
        gate_out[:, columns] = held_mlp[j, :, :960].astype(F32)
        up_out[:, columns] = held_mlp[j, :, 1024:1984].astype(F32)
        down_out[:, columns] = held_mlp[j, :, 2048:3008].astype(F32)
        total = held[j].astype(F32)
        query_out[:, 320 * j : 320 * j + 320] = total[:, :320]
        keyval_out[:, 64 * j : 64 * j + 64] = total[:, 320:384]
    total = output_home[0].astype(F32)
    for p in range(1, 16):
        total = total + output_home[p].astype(F32)
    output_out[...] = total

    def products(weight, grad):
        return jnp.sum(weight[...].astype(F32) * grad[...], axis=1, keepdims=True)

    one = products(query_ref, query_out) + products(keyval_ref, keyval_out)
    two = products(gate_ref, gate_out) + products(up_ref, up_out)
    gain_out[:, :128] = jnp.broadcast_to(one, (40, 128))
    gain_out[:, 128:] = jnp.broadcast_to(two, (40, 128))
    at = 80 * lax.axis_index(T)
    for mine, other, out in ((block_mine, block_other, block_out), (rows_mine, rows_other, rows_out)):
        out[pl.ds(pl.multiple_of(at, 16), 80), :] = mine[...]
        out[pl.ds(pl.multiple_of(80 - at, 16), 80), :] = other[...]


def owners(home, mlp, output_home, w_query, keyval_half, w_gate, w_up, block, rows):
    wide, narrow = (jax.ShapeDtypeStruct((40, n), F32) for n in (3840, 1280))
    small = jax.ShapeDtypeStruct((40, 256), F32)
    tokens = jax.ShapeDtypeStruct((160, 2560), BF)
    return pl.pallas_call(
        owners_kernel,
        out_shape=(narrow, small, narrow, wide, wide, wide, small, tokens, tokens),
        scratch_shapes=[pltpu.VMEM((4, 40, 384), BF), pltpu.VMEM((4, 40, 3072), BF)],
        compiler_params=VMEM,
        cost_estimate=FREE,
    )(*home, *mlp, output_home, w_query, keyval_half, w_gate, w_up, *block, *rows)


def turned(values, cosine, sine):
    one, two = values[:, :64], values[:, 64:128]
    return jnp.concatenate(
        [one * cosine - two * sine, two * cosine + one * sine, values[:, 128:]], axis=1
    )


def prepare_kernel(scale, home_ref, cosine_ref, sine_ref, query_ref, kv_ref, wide):
    cosine, sine = cosine_ref[...], sine_ref[...]
    for j in range(4):
        wide[:, 320 * j : 320 * j + 320] = home_ref[j, :, :320].astype(F32)
    for h in range(5):
        head = turned(wide[:, 256 * h : 256 * h + 256], cosine, sine)
        query_ref[h] = (head * scale).astype(BF)
    for j in range(4):
        wide[:, 64 * j : 64 * j + 64] = home_ref[j, :, 320:].astype(F32)
    first = lax.axis_index(T) == 0
    kv = wide[:, :256]
    kv = jnp.where(first, turned(kv, cosine, sine), kv).astype(BF)
    at = 80 * lax.axis_index(T)
    kv_ref[pl.ds(pl.multiple_of(at, 16), 80), :] = kv[:80]
    kv_ref[pl.ds(pl.multiple_of(80 - at, 16), 80), :] = kv[80:]


def prepare(home, cosine, sine, scale):
    return pl.pallas_call(
        functools.partial(prepare_kernel, scale),
        out_shape=(
            jax.ShapeDtypeStruct((5, 160, 256), BF),
            jax.ShapeDtypeStruct((160, 256), BF),
        ),
        scratch_shapes=[pltpu.VMEM((160, 1280), F32)],
        compiler_params=VMEM,
        cost_estimate=FREE,
    )(home, cosine, sine)


def unturn_kernel(scale, grad_ref, cosine_ref, sine_ref, out_ref, wide):
    cosine, sine = cosine_ref[...], -sine_ref[...]
    for h in range(5):
        wide[:, 256 * h : 256 * h + 256] = turned(grad_ref[h] * scale, cosine, sine)
    for j in range(4):
        out_ref[j] = wide[:, 320 * j : 320 * j + 320].astype(BF)


def unturn(grad, cosine, sine, scale):
    return pl.pallas_call(
        functools.partial(unturn_kernel, scale),
        out_shape=jax.ShapeDtypeStruct((4, 160, 320), BF),
        scratch_shapes=[pltpu.VMEM((160, 1280), F32)],
        compiler_params=VMEM,
        cost_estimate=FREE,
    )(grad, cosine, sine)


def unturn_kv_kernel(home_ref, cosine_ref, sine_ref, out_ref, held):
    total = home_ref[0].astype(F32)
    for p in range(1, 16):
        total = total + home_ref[p].astype(F32)
    held[...] = total
    at = 80 * lax.axis_index(T)
    total = jnp.concatenate(
        [held[pl.ds(pl.multiple_of(at, 16), 80), :], held[pl.ds(pl.multiple_of(80 - at, 16), 80), :]]
    )
    back = turned(total, cosine_ref[...], -sine_ref[...])
    total = jnp.where(lax.axis_index(T) == 0, back, total).astype(BF)
    for j in range(4):
        out_ref[j] = total[:, 64 * j : 64 * j + 64]


def unturn_kv(home, cosine, sine):
    return pl.pallas_call(
        unturn_kv_kernel,
        out_shape=jax.ShapeDtypeStruct((4, 160, 64), BF),
        scratch_shapes=[pltpu.VMEM((160, 256), F32)],
        compiler_params=VMEM,
        cost_estimate=FREE,
    )(home, cosine, sine)


def pieces_kernel(home_ref, out_ref):
    total = home_ref[0].astype(F32)
    for p in range(1, 16):
        total = total + home_ref[p].astype(F32)
    out_ref[...] = total.astype(BF)


def pieces_sum(home):
    cols = home.shape[2]
    return pl.pallas_call(
        pieces_kernel,
        grid=(2,),
        in_specs=[pl.BlockSpec((16, 80, cols), lambda i: (0, i, 0))],
        out_specs=pl.BlockSpec((80, cols), lambda i: (i, 0)),
        out_shape=jax.ShapeDtypeStruct((160, cols), BF),
        compiler_params=VMEM,
        cost_estimate=FREE,
    )(home)


def token_order_kernel(x_ref, out_ref):
    for j in range(4):
        for p in range(16):
            to, at = 40 * (16 * j + p), 40 * (4 * p + j)
            out_ref[:, to : to + 40] = x_ref[:, at : at + 40].astype(BF)


def from_piece_order(x):
    return pl.pallas_call(
        token_order_kernel, out_shape=jax.ShapeDtypeStruct(x.shape, BF), compiler_params=VMEM, cost_estimate=FREE
    )(x)


def shards(
    tokens,
    lengths,
    attn_gain,
    w_query,
    w_keyval,
    w_output,
    mlp_gain,
    w_gate,
    w_up,
    w_down,
    cotangent,
):
    t = lax.axis_index(T)
    me = lax.axis_index(Y)
    piece = lax.axis_index(CONTEXT)
    head_dim = 256
    query_scale = head_dim ** (-0.5)
    seq_count = 2560
    padding = seq_count - lengths[0]
    row_start = piece * 160
    turned_index = row_start + (jnp.arange(160, dtype=jnp.int32) + t * 80) % 160
    live_turned = turned_index >= padding
    live_mine = live_turned[:80, None]

    x_low = to_piece_order(lax.dynamic_slice_in_dim(tokens[0], t * 80, 80, 0))
    cot_mine = to_piece_order(lax.dynamic_slice_in_dim(cotangent[0], t * 80, 80, 0))
    grad_mine = jnp.where(live_mine, cot_mine, jnp.zeros_like(cot_mine))
    x_mine = x_low.astype(F32)
    x_blocks = ring_blocks(x_low, Y)
    w_out = lax.all_gather(w_output, PIECES, axis=0, tiled=True)

    keyval_half = lax.dynamic_slice_in_dim(w_keyval, t * 256, 256, 1)
    gains = jnp.concatenate([attn_gain, mlp_gain])[None, :]
    gains = jnp.pad(gains, ((0, 7), (0, 48)))
    attn_blocks = pack_attention(w_query, keyval_half, gains)
    attn_rows = place(to_owners(attn_blocks), Y, sign=-1)
    attn_copies = jnp.broadcast_to(attn_rows[None], (16, 4, 48, 384))
    attn_all = exchange(attn_copies, CONTEXT).reshape(64, 48, 384)
    w_qkv = attn_all[:, :40].reshape(2560, 384)
    gain_one = attn_all[:, 40, :40].reshape(1, 2560).astype(F32)
    gain_two = attn_all[:, 40, 40:80].reshape(1, 2560).astype(F32)
    x_own = place(x_blocks, Y, attn_all)
    x_other = shift(x_own, T, 1)
    mlp_blocks = pack_mlp(w_gate, w_up, w_down)
    mlp_got = to_owners(mlp_blocks)
    mlp_block = place(mlp_got, Y, x_own, sign=-1).reshape(160, 3072)
    w_mlp = lax.all_gather(mlp_block, CONTEXT, axis=0, tiled=True)

    normed, projected = project(x_own, x_other, gain_one, w_qkv)
    home = exchange(projected, Y)
    cosine, sine = angles(turned_index - padding, head_dim)
    queries, kv_own = prepare(home, cosine, sine, query_scale)
    kv_mine = exchange(jnp.broadcast_to(kv_own[None], (16, 160, 256)), CONTEXT).reshape(2560, 256)
    grad_own = place(ring_blocks(after(grad_mine, kv_own), Y), Y).reshape(320, 2560)
    grad_group = jnp.concatenate([grad_own, shift(grad_own, T, 1)])
    kv_mine = after(kv_mine, grad_own)
    kv_other = shift(kv_mine, T, 1)
    keys = jnp.where(t == 0, kv_mine, kv_other)
    values = jnp.where(t == 0, kv_other, kv_mine)

    key_index = jnp.arange(seq_count, dtype=jnp.int32)
    offset = turned_index[:, None] - key_index[None, :]
    allowed = ((offset >= 0) & (offset < WINDOW) & (key_index >= padding)[None, :])[None]
    live = live_turned[None, :, None]
    scores = jnp.einsum("hqd,kd->hqk", queries, keys, preferred_element_type=F32)
    row_top = jnp.max(jnp.where(allowed, scores, NEGATIVE_FILL), axis=-1, keepdims=True)
    row_top = jnp.where(live, row_top, 0.0)
    weights_exp = jnp.where(allowed, jnp.exp(scores - row_top), 0.0)
    row_total = jnp.where(live, jnp.sum(weights_exp, axis=-1, keepdims=True), 1.0)
    prob = weights_exp / row_total
    prob_low = prob.astype(BF)
    attended = jnp.einsum("hqk,kd->qhd", prob_low, values, preferred_element_type=F32)
    attended = attended.reshape(160, 1280).astype(BF)

    branch = dot(attended, w_out, 1, 1)
    hidden_mine = x_mine + branch[:80] + shift(branch[80:], T, 1)

    inverse_two = inverse_root(hidden_mine)
    normed_two_mine = (hidden_mine * inverse_two * gain_two).astype(BF)
    normed_two = jnp.concatenate(gather_rows(after(normed_two_mine, grad_group)))
    hidden, grad_gate, grad_up = feed_forward(normed_two, grad_group, w_mlp)
    attended_group = place(ring_blocks(attended, Y), Y)
    normed_two_low = core_sum(*row_products((grad_gate, grad_up), w_mlp, 0, 1024, attended_group))
    got = own_and_received(normed_two_low, Y, 0)

    mlp_rows = row_products((hidden,), w_mlp, 2, 1024, normed_two_low)
    down_part = down_grads(grad_group, hidden, *mlp_rows)
    mlp_part = gate_up_grads(normed_two, grad_gate, grad_up, down_part, *got)
    mlp_sum = lax.psum_scatter(mlp_part, CONTEXT, scatter_dimension=0, tiled=True)
    grad_normed_two = sum(block.astype(F32) for block in got)

    grad_h_mine = grad_mine.astype(F32) + norm_back(
        grad_normed_two, hidden_mine, inverse_two, gain_two
    )
    branch_mine = grad_h_mine.astype(BF)
    branch_own = place(to_owners(feature_quarters(grad_h_mine)), Y, sign=-1).reshape(320, 640)
    branch_other = shift(branch_own, T, 1)
    branch_low = jnp.concatenate([branch_mine, shift(branch_mine, T, 1)])
    grad_attended = dot(branch_low, w_out, 1, 0).astype(BF).reshape(160, 5, head_dim)

    grad_prob = jnp.einsum("qhd,kd->hqk", grad_attended, values, preferred_element_type=F32)
    spread = jnp.sum(prob * grad_prob, axis=-1, keepdims=True)
    grad_scores = (prob * (grad_prob - spread)).astype(BF)
    grad_keys = jnp.einsum("hqk,hqd->kd", grad_scores, queries, preferred_element_type=F32)
    grad_values = jnp.einsum("hqk,qhd->kd", prob_low, grad_attended, preferred_element_type=F32)
    keep = jnp.where(t == 0, grad_keys, grad_values)
    give = jnp.where(t == 0, grad_values, grad_keys).astype(BF)
    grad_queries = jnp.einsum("hqk,kd->hqd", grad_scores, keys, preferred_element_type=F32)
    query_blocks = unturn(grad_queries, cosine, sine, query_scale)
    kv_part = (keep + shift(give, T, 1).astype(F32)).astype(BF).reshape(16, 160, 256)
    kv_part = after(kv_part, query_blocks)
    kv_home = exchange(kv_part, CONTEXT)
    grad_query_group = columns_out(query_blocks)
    output_part = outer_output(branch_own, branch_other, attended_group)
    output_home = exchange(after(output_part, kv_home), CONTEXT)
    kv_home = after(kv_home, output_part)
    grad_kv_group = columns_out(unturn_kv(kv_home, cosine, sine))
    grad_qkv = jnp.concatenate([grad_query_group, grad_kv_group], axis=1)
    normed_low = core_sum(*row_products((grad_qkv,), w_qkv, 0, 384))
    part_home = exchange(after(outer(normed, grad_qkv), output_home), CONTEXT)
    (grad_normed,) = sums((own_and_received(normed_low, Y, 0),), (F32,))
    (mlp_mine,) = sums((own_and_received(after(core_sum(*mlp_rows), normed_low), Y, 0),), (F32,))
    inverse_one = inverse_root(x_mine)
    tokens_mine = from_piece_order(
        grad_h_mine + norm_back(grad_normed, x_mine, inverse_one, gain_one)
    )
    block_mine = from_piece_order(jnp.where(live_mine, hidden_mine + mlp_mine, 0.0))
    mlp_home = to_owners(mlp_sum)
    home = to_owners(pieces_sum(part_home))
    query_grad, kv_half, output_grad, gate_grad, up_grad, down_grad, gain_part, block_out, tokens_grad = owners(
        home,
        mlp_home,
        output_home,
        w_query,
        keyval_half,
        w_gate,
        w_up,
        (block_mine, shift(block_mine, T, 1)),
        (tokens_mine, shift(tokens_mine, T, 1)),
    )

    mine = jnp.concatenate([kv_half, gain_part], axis=1)
    other = shift(mine, T, 1)
    kv_other = other[:, :256]
    keyval_grad = jnp.where(
        t == 0,
        jnp.concatenate([kv_half, kv_other], axis=1),
        jnp.concatenate([kv_other, kv_half], axis=1),
    )
    attn_gain_grad = (mine[:, 256] + other[:, 256]) / attn_gain.astype(F32)
    mlp_gain_grad = (mine[:, 384] + other[:, 384]) / mlp_gain.astype(F32)

    return (
        block_out[None],
        tokens_grad[None],
        attn_gain_grad,
        query_grad,
        keyval_grad,
        output_grad,
        mlp_gain_grad,
        gate_grad,
        up_grad,
        down_grad,
    )


def solution(mesh):
    torus = Mesh(
        mesh.devices.reshape(mesh.shape["shard"], 4, 4, mesh.shape["tensor"]),
        ("shard", "context_0", "context_1", "tensor"),
    )
    in_specs = (
        P("shard", CONTEXT, None),
        P("shard"),
        P(SHARD_CONTEXT),
        P(SHARD_CONTEXT, "tensor"),
        P(SHARD_CONTEXT, None),
        P(SHARD_CONTEXT, "tensor"),
        P(SHARD_CONTEXT),
        P(SHARD_CONTEXT, "tensor"),
        P(SHARD_CONTEXT, "tensor"),
        P(SHARD_CONTEXT, "tensor"),
        P("shard", CONTEXT, None),
    )
    out_specs = (
        P("shard", CONTEXT, None),
        P("shard", CONTEXT, None),
        P(SHARD_CONTEXT),
        P(SHARD_CONTEXT, "tensor"),
        P(SHARD_CONTEXT, None),
        P(SHARD_CONTEXT, "tensor"),
        P(SHARD_CONTEXT),
        P(SHARD_CONTEXT, "tensor"),
        P(SHARD_CONTEXT, "tensor"),
        P(SHARD_CONTEXT, "tensor"),
    )
    return jax.shard_map(
        shards, mesh=torus, in_specs=in_specs, out_specs=out_specs, check_vma=False
    )
```

profile of v0, /device:TPU:3, one launch (start us, length us, event | category | flops | bytes accessed | tf_op | source)
XLA Modules:
  0.0 470.9 jit_solution(9148544802499088666)
XLA Ops:
  19.1 7.9 %all-to-all-start = ((bf16[16,4,48,384]{3,2,1,0:T(8,128)(2,1)}), bf16[16,4,48,384]{3,2,1,0:T(8,128)(2,1)S(1)}, u32[]{:S(2)}, u32[]{:S(2)}) async-start(bf16[16,4,48,384]{3,2,1,0:T(8,128)(2,1)} %broadcast_in_dim.94), calls=%async_computation | async-start | bytes 4718592 | tf_op jit(solution)/shard_map/all_to_all | solution.py:32
  44.4 6.6 %collective-permute-done.1.refs_2_ = bf16[80,2560]{1,0:T(8,128)(2,1)S(1)} collective-permute-done((bf16[80,2560]{1,0:T(8,128)(2,1)S(1)}, bf16[80,2560]{1,0:T(8,128)(2,1)S(1)}, u32[]{:S(2)}, u32[]{:S(2)}) %collective-permute-start.1) | collective-permute-done | bytes 409632 | tf_op jit(solution)/shard_map/ppermute | solution.py:28
  58.2 5.5 %collective-permute-done.19.refs_3_ = bf16[40,3072]{1,0:T(8,128)(2,1)S(1)} collective-permute-done((bf16[40,3072]{1,0:T(8,128)(2,1)}, bf16[40,3072]{1,0:T(8,128)(2,1)S(1)}, u32[]{:S(2)}, u32[]{:S(2)}) %collective-permute-start.19) | collective-permute-done | bytes 245792 | tf_op jit(solution)/shard_map/ppermute | solution.py:28
  67.1 6.2 %collective-permute-start.6 = (bf16[4,80,2560]{2,1,0:T(8,128)(2,1)}, bf16[4,80,2560]{2,1,0:T(8,128)(2,1)}, u32[]{:S(2)}, u32[]{:S(2)}) collective-permute-start(bf16[4,80,2560]{2,1,0:T(8,128)(2,1)} %copy-done.6), channel_id=1, source_target_pairs={{0,1},{1,0},{2,3},{3,2},{4,5},{5,4},{6,7},{7,6},{8,9},{9,8},{10,11... | collective-permute-start | bytes 4915208 | tf_op jit(solution)/shard_map/ppermute | solution.py:28
  79.7 5.7 %shard_map.189 = (bf16[2,320,2560]{2,1,0:T(8,128)(2,1)}, bf16[4,160,384]{2,1,0:T(8,128)(2,1)}) custom-call(bf16[4,80,2560]{2,1,0:T(8,128)(2,1)S(1)} %copy-done.7, bf16[4,80,2560]{2,1,0:T(8,128)(2,1)} %collective-permute-done.6.other_ref, f32[1,2560]{1,0:T(1,128)S(1)} %reshape.297.gain_ref, bf16[2560,384]{1,0:T(8,128)(2,1)S(1)} %bitcast.174), custom_call_target="tpu_custom_call" | custom-call | tf_op jit(solution)/shard_map/pallas_call | solution.py:373
  89.9 13.5 %all-to-all-done.1.home_ref = bf16[4,160,384]{2,1,0:T(8,128)(2,1)S(1)} async-done(((bf16[4,160,384]{2,1,0:T(8,128)(2,1)}), bf16[4,160,384]{2,1,0:T(8,128)(2,1)S(1)}, u32[]{:S(2)}, u32[]{:S(2)}) %all-to-all-start.1) | async-done | bytes 491552 | tf_op jit(solution)/shard_map/all_to_all | solution.py:32
  105.9 6.6 %all-to-all-start.2 = ((bf16[16,160,256]{2,1,0:T(8,128)(2,1)}), bf16[16,160,256]{2,1,0:T(8,128)(2,1)S(1)}, u32[]{:S(2)}, u32[]{:S(2)}) async-start(bf16[16,160,256]{2,1,0:T(8,128)(2,1)} %broadcast_in_dim.96), calls=%async_computation.2 | async-start | bytes 2621440 | tf_op jit(solution)/shard_map/all_to_all | solution.py:32
  119.1 8.3 %collective-permute-done.9.refs_3_ = bf16[80,2560]{1,0:T(8,128)(2,1)S(1)} collective-permute-done((bf16[80,2560]{1,0:T(8,128)(2,1)S(1)}, bf16[80,2560]{1,0:T(8,128)(2,1)S(1)}, u32[]{:S(2)}, u32[]{:S(2)}) %collective-permute-start.9) | collective-permute-done | bytes 409632 | tf_op jit(solution)/shard_map/ppermute | solution.py:28
  127.3 7.5 %collective-permute-done.8.refs_2_ = bf16[80,2560]{1,0:T(8,128)(2,1)S(1)} collective-permute-done((bf16[80,2560]{1,0:T(8,128)(2,1)S(1)}, bf16[80,2560]{1,0:T(8,128)(2,1)S(1)}, u32[]{:S(2)}, u32[]{:S(2)}) %collective-permute-start.8) | collective-permute-done | bytes 409632 | tf_op jit(solution)/shard_map/ppermute | solution.py:28
  151.4 5.7 %fusion.52 = f32[160,2560]{1,0:T(8,128)S(1)} fusion(bf16[160,1280]{1,0:T(8,128)(2,1)} %bitcast.189, bf16[2560,1280]{1,0:T(8,128)(2,1)} %all-gather.3.cloned.1.call-done), kind=kOutput, calls=%fused_computation.137 | convolution fusion | flops 1048576000 | bytes 8601600 | tf_op jit(solution)/shard_map/dot_general | solution.py:344
  169.3 9.5 %collective-permute-done.15.refs_3_ = bf16[80,2560]{1,0:T(8,128)(2,1)S(1)} collective-permute-done((bf16[80,2560]{1,0:T(8,128)(2,1)S(1)}, bf16[80,2560]{1,0:T(8,128)(2,1)S(1)}, u32[]{:S(2)}, u32[]{:S(2)}) %collective-permute-start.15) | collective-permute-done | bytes 409632 | tf_op jit(solution)/shard_map/ppermute | solution.py:28
  178.8 8.7 %collective-permute-done.14.refs_2_ = bf16[80,2560]{1,0:T(8,128)(2,1)S(1)} collective-permute-done((bf16[80,2560]{1,0:T(8,128)(2,1)S(1)}, bf16[80,2560]{1,0:T(8,128)(2,1)S(1)}, u32[]{:S(2)}, u32[]{:S(2)}) %collective-permute-start.14) | collective-permute-done | bytes 409632 | tf_op jit(solution)/shard_map/ppermute | solution.py:28
  193.0 8.7 %collective-permute-done.22.refs_3_ = bf16[160,1280]{1,0:T(8,128)(2,1)S(1)} collective-permute-done((bf16[160,1280]{1,0:T(8,128)(2,1)S(1)}, bf16[160,1280]{1,0:T(8,128)(2,1)S(1)}, u32[]{:S(2)}, u32[]{:S(2)}) %collective-permute-start.22) | collective-permute-done | bytes 409632 | tf_op jit(solution)/shard_map/ppermute | solution.py:28
  201.7 9.2 %collective-permute-done.21.refs_2_ = bf16[160,1280]{1,0:T(8,128)(2,1)S(1)} collective-permute-done((bf16[160,1280]{1,0:T(8,128)(2,1)S(1)}, bf16[160,1280]{1,0:T(8,128)(2,1)S(1)}, u32[]{:S(2)}, u32[]{:S(2)}) %collective-permute-start.21) | collective-permute-done | bytes 409632 | tf_op jit(solution)/shard_map/ppermute | solution.py:28
  214.2 6.0 %all-gather.5.cloned.1.call-done.gate_ref.up_ref.down_ref.refs_2_.refs_3_.refs_1_ = bf16[2560,3072]{1,0:T(8,128)(2,1)} async-done(((bf16[160,3072]{1,0:T(8,128)(2,1)}), bf16[2560,3072]{1,0:T(8,128)(2,1)}) %all-gather.5.cloned.1.call-update) | async-done | bytes 15728656 | tf_op jit(solution)/shard_map/all_gather | solution.py:604
  220.2 16.0 %shard_map.198 = (bf16[640,1024]{1,0:T(8,128)(2,1)S(1)}, bf16[640,1024]{1,0:T(8,128)(2,1)S(1)}, bf16[640,1024]{1,0:T(8,128)(2,1)S(1)}) custom-call(bf16[640,2560]{1,0:T(8,128)(2,1)} %pad_maximum_fusion.1.x_ref, bf16[640,2560]{1,0:T(8,128)(2,1)} %copy-done.2, bf16[2560,3072]{1,0:T(8,128)(2,1)} %all-gather.5.cloned.1.call-done.gate_ref.up_ref.down_ref.refs_2_.refs_3_.refs_1_, ...), custom_call_target="tpu_custom_call" | custom-call | tf_op jit(solution)/shard_map/pallas_call | solution.py:307
  236.2 9.6 %shard_map.200 = (bf16[320,2560]{1,0:T(8,128)(2,1)S(1)}, bf16[320,2560]{1,0:T(8,128)(2,1)S(1)}) custom-call(bf16[640,1024]{1,0:T(8,128)(2,1)S(1)} %get-tuple-element.36.refs_0_.gate_ref, bf16[640,1024]{1,0:T(8,128)(2,1)S(1)} %get-tuple-element.37.refs_1_.up_ref, ...), custom_call_target="tpu_custom_call" | custom-call | tf_op jit(solution)/shard_map/pallas_call | solution.py:96
  255.1 7.4 %shard_map.214 = (bf16[320,2560]{1,0:T(8,128)(2,1)}, bf16[320,2560]{1,0:T(8,128)(2,1)S(1)}) custom-call(bf16[640,1024]{1,0:T(8,128)(2,1)S(1)} %get-tuple-element.40.refs_0_.hidden_ref, bf16[2560,3072]{1,0:T(8,128)(2,1)} %all-gather.5.cloned.1.call-done.gate_ref.up_ref.down_ref.refs_2_.refs_3_.refs_1_, bf16[4,80,2560]{2,1,0:T(8,128)(2,1)S(1)} %bitcast.177), custom_call_target="tpu_custom_call" | custom-call | tf_op jit(solution)/shard_map/pallas_call | solution.py:96
  262.4 8.7 %shard_map.215.rest_0_ = bf16[2560,3072]{1,0:T(8,128)(2,1)} custom-call(bf16[640,2560]{1,0:T(8,128)(2,1)} %copy-done.2, bf16[640,1024]{1,0:T(8,128)(2,1)S(1)} %get-tuple-element.40.refs_0_.hidden_ref, bf16[320,2560]{1,0:T(8,128)(2,1)} %get-tuple-element.41.rest_0_, bf16[320,2560]{1,0:T(8,128)(2,1)S(1)} %get-tuple-element.42.rest_1_), custom_call_target="tpu_custom_call" | custom-call | tf_op jit(solution)/shard_map/pallas_call | solution.py:248
  272.3 11.7 %shard_map.216 = bf16[2560,3072]{1,0:T(8,128)(2,1)} custom-call(bf16[640,2560]{1,0:T(8,128)(2,1)} %pad_maximum_fusion.1.x_ref, bf16[640,1024]{1,0:T(8,128)(2,1)S(1)} %get-tuple-element.36.refs_0_.gate_ref, bf16[640,1024]{1,0:T(8,128)(2,1)S(1)} %get-tuple-element.37.refs_1_.up_ref, ...), custom_call_target="tpu_custom_call", output_to_operand_aliasing={{}: (3, {})} | custom-call | tf_op jit(solution)/shard_map/pallas_call | solution.py:272
  290.2 4.1 convolution_convert_fusion
  294.3 6.7 %fusion = (f32[5,160]{1,0:T(8,128)S(1)}, f32[2560,160,5]{0,1,2:T(8,128)S(1)}) fusion(f32[5,160]{1,0:T(8,128)S(1)} %broadcast_select_fusion.7, f32[5,160,2560]{2,1,0:T(8,128)} %copy-done.43, f32[5,160]{1,0:T(8,128)S(1)} %broadcast_select_fusion.8, pred[160,2560]{1,0:T(8,128)(4,1)S(1)} %copy-done.48, bf16[20,5,8,256]{3,2,1,0:T(8,128)(2,1)S(1)} %bitcast.216, ...), kind=kOutput, calls=%fused_computation.2 | convolution fusion | flops 1059470592 | bytes 19834240 | tf_op jit(solution)/shard_map/qhd,kd->hqk/dot_general | solution.py:658
  314.2 6.3 %all-to-all-start.3 = ((bf16[16,160,256]{2,1,0:T(8,128)(2,1)}), bf16[16,160,256]{2,1,0:T(8,128)(2,1)S(1)}, u32[]{:S(2)}, u32[]{:S(2)}) async-start(bf16[16,160,256]{2,1,0:T(8,128)(2,1)} %shard_map.203), calls=%async_computation.3 | async-start | bytes 2621440 | tf_op jit(solution)/shard_map/all_to_all | solution.py:32
  338.8 13.8 %all-to-all-done.3.refs_0_.refs_1_ = bf16[16,160,256]{2,1,0:T(8,128)(2,1)S(1)} async-done(((bf16[16,160,256]{2,1,0:T(8,128)(2,1)}), bf16[16,160,256]{2,1,0:T(8,128)(2,1)S(1)}, u32[]{:S(2)}, u32[]{:S(2)}) %all-to-all-start.3) | async-done | bytes 1310752 | tf_op jit(solution)/shard_map/all_to_all | solution.py:32
  368.3 4.3 all-to-all-start.4
  381.9 3.9 shard_map.210.refs_0_
  385.8 7.2 %all-to-all-done.4.refs_1_.refs_8_ = bf16[16,40,1280]{2,1,0:T(8,128)(2,1)S(1)} async-done(((bf16[16,40,1280]{2,1,0:T(8,128)(2,1)}), bf16[16,40,1280]{2,1,0:T(8,128)(2,1)S(1)}, u32[]{:S(2)}, u32[]{:S(2)}) %all-to-all-start.4) | async-done | bytes 1638432 | tf_op jit(solution)/shard_map/all_to_all | solution.py:32
  393.1 6.5 %all-to-all-start.5 = ((bf16[16,160,384]{2,1,0:T(8,128)(2,1)}), bf16[16,160,384]{2,1,0:T(8,128)(2,1)}, u32[]{:S(2)}, u32[]{:S(2)}) async-start(bf16[16,160,384]{2,1,0:T(8,128)(2,1)} %shard_map.212), calls=%async_computation.5 | async-start | bytes 3932160 | tf_op jit(solution)/shard_map/all_to_all | solution.py:32
  412.2 10.3 %collective-permute-done.48.refs_2_ = bf16[80,2560]{1,0:T(8,128)(2,1)S(1)} collective-permute-done((bf16[80,2560]{1,0:T(8,128)(2,1)S(1)}, bf16[80,2560]{1,0:T(8,128)(2,1)S(1)}, u32[]{:S(2)}, u32[]{:S(2)}) %collective-permute-start.48) | collective-permute-done | bytes 409632 | tf_op jit(solution)/shard_map/ppermute | solution.py:28
  425.3 8.7 %reduce-scatter.2.cloned.1.call-done = bf16[160,3072]{1,0:T(8,128)(2,1)} async-done(((bf16[2560,3072]{1,0:T(8,128)(2,1)}), bf16[160,3072]{1,0:T(8,128)(2,1)}) %reduce-scatter.2.cloned.1.call-update) | async-done | bytes 983056 | tf_op jit(solution)/shard_map/reduce_scatter | solution.py:646
  444.9 4.8 %collective-permute-done.41.refs_3_ = bf16[40,384]{1,0:T(8,128)(2,1)S(1)} collective-permute-done((bf16[40,384]{1,0:T(8,128)(2,1)S(1)}, bf16[40,384]{1,0:T(8,128)(2,1)S(1)}, u32[]{:S(2)}, u32[]{:S(2)}) %collective-permute-start.41) | collective-permute-done | bytes 30752 | tf_op jit(solution)/shard_map/ppermute | solution.py:28
  455.0 3.8 shard_map.223
  (338 shorter events, 205.7 us)
Async XLA Ops:
  7.2 144.2 %all-gather.3.cloned.1.call-start = ((), (), s32[]{:S(2)}) async-start(), calls=%async_computation.7 | async-start | bytes 6656000 | tf_op jit(solution)/shard_map/all_gather | solution.py:587
  19.1 35.7 %all-to-all-start = ((bf16[16,4,48,384]{3,2,1,0:T(8,128)(2,1)}), bf16[16,4,48,384]{3,2,1,0:T(8,128)(2,1)S(1)}, u32[]{:S(2)}, u32[]{:S(2)}) async-start(bf16[16,4,48,384]{3,2,1,0:T(8,128)(2,1)} %broadcast_in_dim.94), calls=%async_computation | async-start | bytes 4718592 | tf_op jit(solution)/shard_map/all_to_all | solution.py:32
  26.9 193.2 %all-gather.5.cloned.1.call-start = ((), (), s32[]{:S(2)}) async-start(), calls=%async_computation.8 | async-start | bytes 16711680 | tf_op jit(solution)/shard_map/all_gather | solution.py:604
  34.6 19.5 %collective-permute-start = (bf16[80,2560]{1,0:T(8,128)(2,1)S(1)}, bf16[80,2560]{1,0:T(8,128)(2,1)S(1)}, u32[]{:S(2)}, u32[]{:S(2)}) collective-permute-start(bf16[80,2560]{1,0:T(8,128)(2,1)S(1)} %copy.40.refs_0_), channel_id=1, source_target_pairs={{0,96},{32,0},{64,32},{96,64},{1,97},{33,1},{65,33},{97,65},{2,98}... | collective-permute-start | bytes 1228808 | tf_op jit(solution)/shard_map/ppermute | solution.py:28
  39.3 24.4 %collective-permute-start.19 = (bf16[40,3072]{1,0:T(8,128)(2,1)}, bf16[40,3072]{1,0:T(8,128)(2,1)S(1)}, u32[]{:S(2)}, u32[]{:S(2)}) collective-permute-start(bf16[40,3072]{1,0:T(8,128)(2,1)} %get-tuple-element.79), channel_id=1, source_target_pairs={{0,96},{32,0},{64,32},{96,64},{1,97},{33,1},{65,33},{97,65},{2,98}... | collective-permute-start | bytes 737288 | tf_op jit(solution)/shard_map/ppermute | solution.py:28
  39.3 24.4 %collective-permute-start.18 = (bf16[40,3072]{1,0:T(8,128)(2,1)}, bf16[40,3072]{1,0:T(8,128)(2,1)}, u32[]{:S(2)}, u32[]{:S(2)}) collective-permute-start(bf16[40,3072]{1,0:T(8,128)(2,1)} %get-tuple-element.80), channel_id=1, source_target_pairs={{0,64},{32,96},{64,0},{96,32},{1,65},{33,97},{65,1},{97,33},{2,66}... | collective-permute-start | bytes 737288 | tf_op jit(solution)/shard_map/ppermute | solution.py:28
  44.4 19.3 %collective-permute-start.17 = (bf16[40,3072]{1,0:T(8,128)(2,1)}, bf16[40,3072]{1,0:T(8,128)(2,1)}, u32[]{:S(2)}, u32[]{:S(2)}) collective-permute-start(bf16[40,3072]{1,0:T(8,128)(2,1)} %get-tuple-element.81), channel_id=1, source_target_pairs={{0,32},{32,64},{64,96},{96,0},{1,33},{33,65},{65,97},{97,1},{2,34}... | collective-permute-start | bytes 737288 | tf_op jit(solution)/shard_map/ppermute | solution.py:28
  105.9 31.1 %all-to-all-start.2 = ((bf16[16,160,256]{2,1,0:T(8,128)(2,1)}), bf16[16,160,256]{2,1,0:T(8,128)(2,1)S(1)}, u32[]{:S(2)}, u32[]{:S(2)}) async-start(bf16[16,160,256]{2,1,0:T(8,128)(2,1)} %broadcast_in_dim.96), calls=%async_computation.2 | async-start | bytes 2621440 | tf_op jit(solution)/shard_map/all_to_all | solution.py:32
  112.5 321.5 %reduce-scatter.2.cloned.1.call-start = ((), (), s32[]{:S(2)}) async-start(), calls=%async_computation.9 | async-start | bytes 16711680 | tf_op jit(solution)/shard_map/reduce_scatter | solution.py:646
  116.6 18.3 %collective-permute-start.8 = (bf16[80,2560]{1,0:T(8,128)(2,1)S(1)}, bf16[80,2560]{1,0:T(8,128)(2,1)S(1)}, u32[]{:S(2)}, u32[]{:S(2)}) collective-permute-start(bf16[80,2560]{1,0:T(8,128)(2,1)S(1)} %shard_map.191.refs_0_), channel_id=1, source_target_pairs={{0,64},{32,96},{64,0},{96,32},{1,65},{33,97},{65,1},{97,33},{2,66}... | collective-permute-start | bytes 1228808 | tf_op jit(solution)/shard_map/ppermute | solution.py:28
  118.3 18.5 %collective-permute-start.7 = (bf16[80,2560]{1,0:T(8,128)(2,1)S(1)}, bf16[80,2560]{1,0:T(8,128)(2,1)S(1)}, u32[]{:S(2)}, u32[]{:S(2)}) collective-permute-start(bf16[80,2560]{1,0:T(8,128)(2,1)S(1)} %shard_map.191.refs_0_), channel_id=1, source_target_pairs={{0,96},{32,0},{64,32},{96,64},{1,97},{33,1},{65,33},{97,65},{2,98}... | collective-permute-start | bytes 1228808 | tf_op jit(solution)/shard_map/ppermute | solution.py:28
  139.8 21.6 %collective-permute-start.12 = (bf16[320,2560]{1,0:T(8,128)(2,1)S(1)}, bf16[320,2560]{1,0:T(8,128)(2,1)}, u32[]{:S(2)}, u32[]{:S(2)}) collective-permute-start(bf16[320,2560]{1,0:T(8,128)(2,1)S(1)} %bitcast.180), channel_id=1, source_target_pairs={{0,1},{1,0},{2,3},{3,2},{4,5},{5,4},{6,7},{7,6},{8,9},{9,8},{10,11... | collective-permute-start | bytes 4915208 | tf_op jit(solution)/shard_map/ppermute | solution.py:28
  166.6 20.9 %collective-permute-start.14 = (bf16[80,2560]{1,0:T(8,128)(2,1)S(1)}, bf16[80,2560]{1,0:T(8,128)(2,1)S(1)}, u32[]{:S(2)}, u32[]{:S(2)}) collective-permute-start(bf16[80,2560]{1,0:T(8,128)(2,1)S(1)} %shard_map.194.refs_0_), channel_id=1, source_target_pairs={{0,64},{32,96},{64,0},{96,32},{1,65},{33,97},{65,1},{97,33},{2,66}... | collective-permute-start | bytes 1228808 | tf_op jit(solution)/shard_map/ppermute | solution.py:28
  169.2 18.8 %collective-permute-start.13 = (bf16[80,2560]{1,0:T(8,128)(2,1)S(1)}, bf16[80,2560]{1,0:T(8,128)(2,1)S(1)}, u32[]{:S(2)}, u32[]{:S(2)}) collective-permute-start(bf16[80,2560]{1,0:T(8,128)(2,1)S(1)} %shard_map.194.refs_0_), channel_id=1, source_target_pairs={{0,96},{32,0},{64,32},{96,64},{1,97},{33,1},{65,33},{97,65},{2,98}... | collective-permute-start | bytes 1228808 | tf_op jit(solution)/shard_map/ppermute | solution.py:28
  188.0 24.2 %collective-permute-start.16 = (bf16[320,2560]{1,0:T(8,128)(2,1)S(1)}, bf16[320,2560]{1,0:T(8,128)(2,1)S(1)}, u32[]{:S(2)}, u32[]{:S(2)}) collective-permute-start(bf16[320,2560]{1,0:T(8,128)(2,1)S(1)} %bitcast.186), channel_id=1, source_target_pairs={{0,1},{1,0},{2,3},{3,2},{4,5},{5,4},{6,7},{7,6},{8,9},{9,8},{10,11... | collective-permute-start | bytes 4915208 | tf_op jit(solution)/shard_map/ppermute | solution.py:28
  189.3 21.6 %collective-permute-start.21 = (bf16[160,1280]{1,0:T(8,128)(2,1)S(1)}, bf16[160,1280]{1,0:T(8,128)(2,1)S(1)}, u32[]{:S(2)}, u32[]{:S(2)}) collective-permute-start(bf16[160,1280]{1,0:T(8,128)(2,1)S(1)} %bitcast.191), channel_id=1, source_target_pairs={{0,64},{32,96},{64,0},{96,32},{1,65},{33,97},{65,1},{97,33},{2,66}... | collective-permute-start | bytes 1228808 | tf_op jit(solution)/shard_map/ppermute | solution.py:28
  192.6 18.3 %collective-permute-start.20 = (bf16[160,1280]{1,0:T(8,128)(2,1)S(1)}, bf16[160,1280]{1,0:T(8,128)(2,1)S(1)}, u32[]{:S(2)}, u32[]{:S(2)}) collective-permute-start(bf16[160,1280]{1,0:T(8,128)(2,1)S(1)} %bitcast.192), channel_id=1, source_target_pairs={{0,96},{32,0},{64,32},{96,64},{1,97},{33,1},{65,33},{97,65},{2,98}... | collective-permute-start | bytes 1228808 | tf_op jit(solution)/shard_map/ppermute | solution.py:28
  250.2 20.9 %collective-permute-start.24 = (bf16[80,2560]{1,0:T(8,128)(2,1)S(1)}, bf16[80,2560]{1,0:T(8,128)(2,1)S(1)}, u32[]{:S(2)}, u32[]{:S(2)}) collective-permute-start(bf16[80,2560]{1,0:T(8,128)(2,1)S(1)} %get-tuple-element.72), channel_id=1, source_target_pairs={{0,32},{32,64},{64,96},{96,0},{1,33},{33,65},{65,97},{97,1},{2,34}... | collective-permute-start | bytes 1228808 | tf_op jit(solution)/shard_map/ppermute | solution.py:28
  251.5 20.4 %collective-permute-start.26 = (bf16[80,2560]{1,0:T(8,128)(2,1)S(1)}, bf16[80,2560]{1,0:T(8,128)(2,1)S(1)}, u32[]{:S(2)}, u32[]{:S(2)}) collective-permute-start(bf16[80,2560]{1,0:T(8,128)(2,1)S(1)} %get-tuple-element.73), channel_id=1, source_target_pairs={{0,64},{32,96},{64,0},{96,32},{1,65},{33,97},{65,1},{97,33},{2,66}... | collective-permute-start | bytes 1228808 | tf_op jit(solution)/shard_map/ppermute | solution.py:28
  314.2 38.4 %all-to-all-start.3 = ((bf16[16,160,256]{2,1,0:T(8,128)(2,1)}), bf16[16,160,256]{2,1,0:T(8,128)(2,1)S(1)}, u32[]{:S(2)}, u32[]{:S(2)}) async-start(bf16[16,160,256]{2,1,0:T(8,128)(2,1)} %shard_map.203), calls=%async_computation.3 | async-start | bytes 2621440 | tf_op jit(solution)/shard_map/all_to_all | solution.py:32
  333.2 22.6 %collective-permute-start.30 = (bf16[160,320]{1,0:T(8,128)(2,1)}, bf16[160,320]{1,0:T(8,128)(2,1)}, u32[]{:S(2)}, u32[]{:S(2)}) collective-permute-start(bf16[160,320]{1,0:T(8,128)(2,1)} %get-tuple-element.83), channel_id=1, source_target_pairs={{0,96},{32,0},{64,32},{96,64},{1,97},{33,1},{65,33},{97,65},{2,98}... | collective-permute-start | bytes 307208 | tf_op jit(solution)/shard_map/ppermute | solution.py:28
  333.5 22.5 %collective-permute-start.29 = (bf16[160,320]{1,0:T(8,128)(2,1)}, bf16[160,320]{1,0:T(8,128)(2,1)}, u32[]{:S(2)}, u32[]{:S(2)}) collective-permute-start(bf16[160,320]{1,0:T(8,128)(2,1)} %get-tuple-element.84), channel_id=1, source_target_pairs={{0,64},{32,96},{64,0},{96,32},{1,65},{33,97},{65,1},{97,33},{2,66}... | collective-permute-start | bytes 307208 | tf_op jit(solution)/shard_map/ppermute | solution.py:28
  334.4 21.7 %collective-permute-start.28 = (bf16[160,320]{1,0:T(8,128)(2,1)}, bf16[160,320]{1,0:T(8,128)(2,1)}, u32[]{:S(2)}, u32[]{:S(2)}) collective-permute-start(bf16[160,320]{1,0:T(8,128)(2,1)} %get-tuple-element.85), channel_id=1, source_target_pairs={{0,32},{32,64},{64,96},{96,0},{1,33},{33,65},{65,97},{97,1},{2,34}... | collective-permute-start | bytes 307208 | tf_op jit(solution)/shard_map/ppermute | solution.py:28
  368.3 24.8 %all-to-all-start.4 = ((bf16[16,40,1280]{2,1,0:T(8,128)(2,1)}), bf16[16,40,1280]{2,1,0:T(8,128)(2,1)S(1)}, u32[]{:S(2)}, u32[]{:S(2)}) async-start(bf16[16,40,1280]{2,1,0:T(8,128)(2,1)} %shard_map.211), calls=%async_computation.4 | async-start | bytes 3276800 | tf_op jit(solution)/shard_map/all_to_all | solution.py:32
  376.2 29.0 %collective-permute-start.53 = (bf16[80,2560]{1,0:T(8,128)(2,1)}, bf16[80,2560]{1,0:T(8,128)(2,1)}, u32[]{:S(2)}, u32[]{:S(2)}) collective-permute-start(bf16[80,2560]{1,0:T(8,128)(2,1)} %get-tuple-element.64), channel_id=1, source_target_pairs={{0,64},{32,96},{64,0},{96,32},{1,65},{33,97},{65,1},{97,33},{2,66}... | collective-permute-start | bytes 1228808 | tf_op jit(solution)/shard_map/ppermute | solution.py:28
  377.1 29.4 %collective-permute-start.52 = (bf16[80,2560]{1,0:T(8,128)(2,1)}, bf16[80,2560]{1,0:T(8,128)(2,1)}, u32[]{:S(2)}, u32[]{:S(2)}) collective-permute-start(bf16[80,2560]{1,0:T(8,128)(2,1)} %get-tuple-element.65), channel_id=1, source_target_pairs={{0,96},{32,0},{64,32},{96,64},{1,97},{33,1},{65,33},{97,65},{2,98}... | collective-permute-start | bytes 1228808 | tf_op jit(solution)/shard_map/ppermute | solution.py:28
  377.8 28.7 %collective-permute-start.51 = (bf16[80,2560]{1,0:T(8,128)(2,1)}, bf16[80,2560]{1,0:T(8,128)(2,1)}, u32[]{:S(2)}, u32[]{:S(2)}) collective-permute-start(bf16[80,2560]{1,0:T(8,128)(2,1)} %get-tuple-element.66), channel_id=1, source_target_pairs={{0,32},{32,64},{64,96},{96,0},{1,33},{33,65},{65,97},{97,1},{2,34}... | collective-permute-start | bytes 1228808 | tf_op jit(solution)/shard_map/ppermute | solution.py:28
  393.1 46.7 %all-to-all-start.5 = ((bf16[16,160,384]{2,1,0:T(8,128)(2,1)}), bf16[16,160,384]{2,1,0:T(8,128)(2,1)}, u32[]{:S(2)}, u32[]{:S(2)}) async-start(bf16[16,160,384]{2,1,0:T(8,128)(2,1)} %shard_map.212), calls=%async_computation.5 | async-start | bytes 3932160 | tf_op jit(solution)/shard_map/all_to_all | solution.py:32
  405.2 18.2 %collective-permute-start.47 = (bf16[80,2560]{1,0:T(8,128)(2,1)S(1)}, bf16[80,2560]{1,0:T(8,128)(2,1)S(1)}, u32[]{:S(2)}, u32[]{:S(2)}) collective-permute-start(bf16[80,2560]{1,0:T(8,128)(2,1)S(1)} %get-tuple-element.70), channel_id=1, source_target_pairs={{0,32},{32,64},{64,96},{96,0},{1,33},{33,65},{65,97},{97,1},{2,34}... | collective-permute-start | bytes 1228808 | tf_op jit(solution)/shard_map/ppermute | solution.py:28
  409.3 32.1 %collective-permute-start.54 = (bf16[80,2560]{1,0:T(8,128)(2,1)S(1)}, bf16[80,2560]{1,0:T(8,128)(2,1)}, u32[]{:S(2)}, u32[]{:S(2)}) collective-permute-start(bf16[80,2560]{1,0:T(8,128)(2,1)S(1)} %shard_map.222.refs_15_), channel_id=1, source_target_pairs={{0,1},{1,0},{2,3},{3,2},{4,5},{5,4},{6,7},{7,6},{8,9},{9,8},{10,11... | collective-permute-start | bytes 1228808 | tf_op jit(solution)/shard_map/ppermute | solution.py:28
  424.6 19.1 %collective-permute-start.50 = (bf16[80,2560]{1,0:T(8,128)(2,1)S(1)}, bf16[80,2560]{1,0:T(8,128)(2,1)}, u32[]{:S(2)}, u32[]{:S(2)}) collective-permute-start(bf16[80,2560]{1,0:T(8,128)(2,1)S(1)} %shard_map.220.refs_13_), channel_id=1, source_target_pairs={{0,1},{1,0},{2,3},{3,2},{4,5},{5,4},{6,7},{7,6},{8,9},{9,8},{10,11... | collective-permute-start | bytes 1228808 | tf_op jit(solution)/shard_map/ppermute | solution.py:28
  436.2 18.7 %collective-permute-start.44 = (bf16[40,3072]{1,0:T(8,128)(2,1)}, bf16[40,3072]{1,0:T(8,128)(2,1)}, u32[]{:S(2)}, u32[]{:S(2)}) collective-permute-start(bf16[40,3072]{1,0:T(8,128)(2,1)} %get-tuple-element.75), channel_id=1, source_target_pairs={{0,96},{32,0},{64,32},{96,64},{1,97},{33,1},{65,33},{97,65},{2,98}... | collective-permute-start | bytes 737288 | tf_op jit(solution)/shard_map/ppermute | solution.py:28
  (93 other events, 841.9 us)
Sparse Core Ops, SparseCore 0:
  10.9 96.3 all-gather.2
  109.4 110.6 all-gather.4
  284.1 149.8 reduce-scatter.1
where the time goes:
time: 480 us; the launch traced here: 471 us
  waiting for transfers between devices  167 us (35%)
  starting transfers between devices  105 us (22%)
  Pallas kernels  82.2 us (17%)
  local copies, waits for them, and re-layouts  44.7 us (9%)
  matrix products  29.2 us (6%)
  other arithmetic  27.2 us (6%)
  between operations  16 us (3%)
    ppermute x56, waiting for transfers between devices, shift(): return lax.ppermute(x, axis, [(i, (i + by) % n) for i in range(n)])  117 us
    ppermute x56, starting transfers between devices, shift(): return lax.ppermute(x, axis, [(i, (i + by) % n) for i in range(n)])  69.6 us
    all_to_all x6, starting transfers between devices, exchange(): return lax.all_to_all(blocks, axis, 0, 0, tiled=True)  35 us
    all_to_all x6, waiting for transfers between devices, exchange(): return lax.all_to_all(blocks, axis, 0, 0, tiled=True)  34.5 us
    unnamed x123, local copies, waits for them, and re-layouts  26.3 us
    pallas_call x3, Pallas kernels, row_products(): pl.pallas_call(functools.partial(rows_kernel, count), grid=(n // rows,),...  19.9 us
    pallas_call x1, Pallas kernels, feed_forward(): pl.pallas_call(feed_forward_kernel, grid=(steps,), out_shape=(part, part,...  16 us
    pallas_call x1, Pallas kernels, gate_up_grads(): pl.pallas_call(gate_up_grad_kernel, grid=(2560 // rows,), out_shape=jax.S...  11.7 us
  transfers between devices with their start and end apart: 65, of which 37 were waited for; matrix products, arithmetic and copies ran while one was open for 16% of the time, Pallas kernels for 9%

commit v1 on v0

--- a/solution.py
+++ b/solution.py
@@ -239,11 +239,32 @@
     )(w_gate, w_up, w_down)
 
 
+def gate_up_grad_kernel(x_ref, gate_ref, up_ref, *rest):
+    out_ref = rest[-1]
+    out_ref[:, :1024] = dot(x_ref[...], gate_ref[...], 0, 0).astype(BF)
+    out_ref[:, 1024:] = dot(x_ref[...], up_ref[...], 0, 0).astype(BF)
+
+
+def gate_up_grads(normed, gate, up, *first):
+    rows = 512
+    whole = pl.BlockSpec((640, 1024), lambda i: (0, 0))
+    return pl.pallas_call(
+        gate_up_grad_kernel,
+        grid=(2560 // rows,),
+        out_shape=jax.ShapeDtypeStruct((2560, 3072), BF),
+        in_specs=[pl.BlockSpec((640, rows), lambda i: (0, i)), whole, whole]
+        + [ANYWHERE] * len(first),
+        out_specs=pl.BlockSpec((rows, 2048), lambda i: (i, 0)),
+        compiler_params=VMEM,
+        cost_estimate=FREE,
+    )(normed, gate, up, *first)
+
+
 def down_grad_kernel(y_ref, hidden_ref, *rest):
     rest[-1][...] = dot(y_ref[...], hidden_ref[...], 0, 0).astype(BF)
 
 
-def down_grads(grads, hidden, *first):
+def down_grads(grads, hidden, held, *first):
     rows = 512
     return pl.pallas_call(
         down_grad_kernel,
@@ -253,33 +274,12 @@
             pl.BlockSpec((640, rows), lambda i: (0, i)),
             pl.BlockSpec((640, 1024), lambda i: (0, 0)),
         ]
-        + [ANYWHERE] * len(first),
+        + [ANYWHERE] * (1 + len(first)),
         out_specs=pl.BlockSpec((rows, 1024), lambda i: (i, 2)),
-        compiler_params=VMEM,
-        cost_estimate=FREE,
-    )(grads, hidden, *first)
-
-
-def gate_up_grad_kernel(x_ref, gate_ref, up_ref, *rest):
-    out_ref = rest[-1]
-    out_ref[:, :1024] = dot(x_ref[...], gate_ref[...], 0, 0).astype(BF)
-    out_ref[:, 1024:] = dot(x_ref[...], up_ref[...], 0, 0).astype(BF)
-
-
-def gate_up_grads(normed, gate, up, held, *first):
-    rows = 512
-    whole = pl.BlockSpec((640, 1024), lambda i: (0, 0))
-    return pl.pallas_call(
-        gate_up_grad_kernel,
-        grid=(2560 // rows,),
-        out_shape=jax.ShapeDtypeStruct((2560, 3072), BF),
-        in_specs=[pl.BlockSpec((640, rows), lambda i: (0, i)), whole, whole]
-        + [ANYWHERE] * (1 + len(first)),
-        out_specs=pl.BlockSpec((rows, 2048), lambda i: (i, 0)),
-        input_output_aliases={3: 0},
-        compiler_params=VMEM,
-        cost_estimate=FREE,
-    )(normed, gate, up, held, *first)
+        input_output_aliases={2: 0},
+        compiler_params=VMEM,
+        cost_estimate=FREE,
+    )(grads, hidden, held, *first)
 
 
 def feed_forward_kernel(x_ref, y_ref, gate_ref, up_ref, down_ref, *rest):
@@ -640,9 +640,8 @@
     normed_two_low = core_sum(*row_products((grad_gate, grad_up), w_mlp, 0, 1024, attended_group))
     got = own_and_received(normed_two_low, Y, 0)
 
-    mlp_rows = row_products((hidden,), w_mlp, 2, 1024, normed_two_low)
-    down_part = down_grads(grad_group, hidden, *mlp_rows)
-    mlp_part = gate_up_grads(normed_two, grad_gate, grad_up, down_part, *got)
+    gate_up_part = gate_up_grads(normed_two, grad_gate, grad_up, normed_two_low)
+    mlp_part = down_grads(grad_group, hidden, gate_up_part, *got)
     mlp_sum = lax.psum_scatter(mlp_part, CONTEXT, scatter_dimension=0, tiled=True)
     grad_normed_two = sum(block.astype(F32) for block in got)
 
@@ -670,7 +669,8 @@
     grad_query_group = columns_out(query_blocks)
     output_part = outer_output(branch_own, branch_other, attended_group)
     output_home = exchange(after(output_part, kv_home), CONTEXT)
-    kv_home = after(kv_home, output_part)
+    mlp_rows = row_products((hidden,), w_mlp, 2, 1024, output_part)
+    kv_home = after(kv_home, output_part, *mlp_rows)
     grad_kv_group = columns_out(unturn_kv(kv_home, cosine, sine))
     grad_qkv = jnp.concatenate([grad_query_group, grad_kv_group], axis=1)
     normed_low = core_sum(*row_products((grad_qkv,), w_qkv, 0, 384))

time: 480 us -> 476 us (level)
  the two profiles are of different devices: /device:TPU:3 before, /device:TPU:1 now
where the time goes in v1:
time: 476 us; the launch traced here: 466 us
  waiting for transfers between devices  156 us (33%)
  starting transfers between devices  109 us (23%)
  Pallas kernels  80.6 us (17%)
  local copies, waits for them, and re-layouts  47.9 us (10%)
  matrix products  28.9 us (6%)
  other arithmetic  27.1 us (6%)
  between operations  16 us (3%)
    ppermute x56, waiting for transfers between devices, shift(): return lax.ppermute(x, axis, [(i, (i + by) % n) for i in range(n)])  118 us
    ppermute x56, starting transfers between devices, shift(): return lax.ppermute(x, axis, [(i, (i + by) % n) for i in range(n)])  70.5 us
    all_to_all x6, starting transfers between devices, exchange(): return lax.all_to_all(blocks, axis, 0, 0, tiled=True)  38.6 us
    unnamed x131, local copies, waits for them, and re-layouts  29.6 us
    all_to_all x6, waiting for transfers between devices, exchange(): return lax.all_to_all(blocks, axis, 0, 0, tiled=True)  24.5 us
    pallas_call x3, Pallas kernels, row_products(): pl.pallas_call(functools.partial(rows_kernel, count), grid=(n // rows,),...  20.4 us
    pallas_call x1, Pallas kernels, feed_forward(): pl.pallas_call(feed_forward_kernel, grid=(steps,), out_shape=(part, part,...  16 us
    pallas_call x1, Pallas kernels, gate_up_grads(): pl.pallas_call(gate_up_grad_kernel, grid=(2560 // rows,), out_shape=jax.S...  11.8 us
  transfers between devices with their start and end apart: 65, of which 37 were waited for; matrix products, arithmetic and copies ran while one was open for 16% of the time, Pallas kernels for 10%

profile of v1, /device:TPU:1, one launch (start us, length us, event | category | flops | bytes accessed | tf_op | source)
XLA Modules:
  0.0 466.1 jit_solution(16831868302194348736)
XLA Ops:
  9.8 3.6 collective-permute-start.5
  19.9 7.7 %all-to-all-start = ((bf16[16,4,48,384]{3,2,1,0:T(8,128)(2,1)}), bf16[16,4,48,384]{3,2,1,0:T(8,128)(2,1)S(1)}, u32[]{:S(2)}, u32[]{:S(2)}) async-start(bf16[16,4,48,384]{3,2,1,0:T(8,128)(2,1)} %broadcast_in_dim.94), calls=%async_computation | async-start | bytes 4718592 | tf_op jit(solution)/shard_map/all_to_all | solution.py:32
  44.4 7.5 %collective-permute-done.1.refs_2_ = bf16[80,2560]{1,0:T(8,128)(2,1)S(1)} collective-permute-done((bf16[80,2560]{1,0:T(8,128)(2,1)S(1)}, bf16[80,2560]{1,0:T(8,128)(2,1)S(1)}, u32[]{:S(2)}, u32[]{:S(2)}) %collective-permute-start.1) | collective-permute-done | bytes 409632 | tf_op jit(solution)/shard_map/ppermute | solution.py:28
  66.4 6.9 %collective-permute-start.6 = (bf16[4,80,2560]{2,1,0:T(8,128)(2,1)}, bf16[4,80,2560]{2,1,0:T(8,128)(2,1)}, u32[]{:S(2)}, u32[]{:S(2)}) collective-permute-start(bf16[4,80,2560]{2,1,0:T(8,128)(2,1)} %copy-done.7), channel_id=1, source_target_pairs={{0,1},{1,0},{2,3},{3,2},{4,5},{5,4},{6,7},{7,6},{8,9},{9,8},{10,11... | collective-permute-start | bytes 4915208 | tf_op jit(solution)/shard_map/ppermute | solution.py:28
  79.8 5.7 %shard_map.189 = (bf16[2,320,2560]{2,1,0:T(8,128)(2,1)}, bf16[4,160,384]{2,1,0:T(8,128)(2,1)}) custom-call(bf16[4,80,2560]{2,1,0:T(8,128)(2,1)S(1)} %copy-done.8, bf16[4,80,2560]{2,1,0:T(8,128)(2,1)} %collective-permute-done.6.other_ref, f32[1,2560]{1,0:T(1,128)S(1)} %reshape.297.gain_ref, bf16[2560,384]{1,0:T(8,128)(2,1)S(1)} %bitcast.174), custom_call_target="tpu_custom_call" | custom-call | tf_op jit(solution)/shard_map/pallas_call | solution.py:373
  90.1 13.2 %all-to-all-done.1.home_ref = bf16[4,160,384]{2,1,0:T(8,128)(2,1)S(1)} async-done(((bf16[4,160,384]{2,1,0:T(8,128)(2,1)}), bf16[4,160,384]{2,1,0:T(8,128)(2,1)S(1)}, u32[]{:S(2)}, u32[]{:S(2)}) %all-to-all-start.1) | async-done | bytes 491552 | tf_op jit(solution)/shard_map/all_to_all | solution.py:32
  105.8 7.3 %all-to-all-start.2 = ((bf16[16,160,256]{2,1,0:T(8,128)(2,1)}), bf16[16,160,256]{2,1,0:T(8,128)(2,1)S(1)}, u32[]{:S(2)}, u32[]{:S(2)}) async-start(bf16[16,160,256]{2,1,0:T(8,128)(2,1)} %broadcast_in_dim.96), calls=%async_computation.2 | async-start | bytes 2621440 | tf_op jit(solution)/shard_map/all_to_all | solution.py:32
  119.8 8.6 %collective-permute-done.9.refs_3_ = bf16[80,2560]{1,0:T(8,128)(2,1)S(1)} collective-permute-done((bf16[80,2560]{1,0:T(8,128)(2,1)S(1)}, bf16[80,2560]{1,0:T(8,128)(2,1)S(1)}, u32[]{:S(2)}, u32[]{:S(2)}) %collective-permute-start.9) | collective-permute-done | bytes 409632 | tf_op jit(solution)/shard_map/ppermute | solution.py:28
  128.3 7.5 %collective-permute-done.8.refs_2_ = bf16[80,2560]{1,0:T(8,128)(2,1)S(1)} collective-permute-done((bf16[80,2560]{1,0:T(8,128)(2,1)S(1)}, bf16[80,2560]{1,0:T(8,128)(2,1)S(1)}, u32[]{:S(2)}, u32[]{:S(2)}) %collective-permute-start.8) | collective-permute-done | bytes 409632 | tf_op jit(solution)/shard_map/ppermute | solution.py:28
  151.7 5.4 %fusion.52 = f32[160,2560]{1,0:T(8,128)S(1)} fusion(bf16[160,1280]{1,0:T(8,128)(2,1)} %bitcast.189, bf16[2560,1280]{1,0:T(8,128)(2,1)} %all-gather.3.cloned.1.call-done), kind=kOutput, calls=%fused_computation.137 | convolution fusion | flops 1048576000 | bytes 8601600 | tf_op jit(solution)/shard_map/dot_general | solution.py:344
  169.4 9.4 %collective-permute-done.15.refs_3_ = bf16[80,2560]{1,0:T(8,128)(2,1)S(1)} collective-permute-done((bf16[80,2560]{1,0:T(8,128)(2,1)S(1)}, bf16[80,2560]{1,0:T(8,128)(2,1)S(1)}, u32[]{:S(2)}, u32[]{:S(2)}) %collective-permute-start.15) | collective-permute-done | bytes 409632 | tf_op jit(solution)/shard_map/ppermute | solution.py:28
  178.8 9.0 %collective-permute-done.14.refs_2_ = bf16[80,2560]{1,0:T(8,128)(2,1)S(1)} collective-permute-done((bf16[80,2560]{1,0:T(8,128)(2,1)S(1)}, bf16[80,2560]{1,0:T(8,128)(2,1)S(1)}, u32[]{:S(2)}, u32[]{:S(2)}) %collective-permute-start.14) | collective-permute-done | bytes 409632 | tf_op jit(solution)/shard_map/ppermute | solution.py:28
  193.1 8.4 %collective-permute-done.22.refs_3_ = bf16[160,1280]{1,0:T(8,128)(2,1)S(1)} collective-permute-done((bf16[160,1280]{1,0:T(8,128)(2,1)S(1)}, bf16[160,1280]{1,0:T(8,128)(2,1)S(1)}, u32[]{:S(2)}, u32[]{:S(2)}) %collective-permute-start.22) | collective-permute-done | bytes 409632 | tf_op jit(solution)/shard_map/ppermute | solution.py:28
  201.5 9.5 %collective-permute-done.21.refs_2_ = bf16[160,1280]{1,0:T(8,128)(2,1)S(1)} collective-permute-done((bf16[160,1280]{1,0:T(8,128)(2,1)S(1)}, bf16[160,1280]{1,0:T(8,128)(2,1)S(1)}, u32[]{:S(2)}, u32[]{:S(2)}) %collective-permute-start.21) | collective-permute-done | bytes 409632 | tf_op jit(solution)/shard_map/ppermute | solution.py:28
  214.3 6.8 %all-gather.5.cloned.1.call-done.gate_ref.up_ref.down_ref.refs_2_.refs_3_.refs_1_ = bf16[2560,3072]{1,0:T(8,128)(2,1)} async-done(((bf16[160,3072]{1,0:T(8,128)(2,1)}), bf16[2560,3072]{1,0:T(8,128)(2,1)}) %all-gather.5.cloned.1.call-update) | async-done | bytes 15728656 | tf_op jit(solution)/shard_map/all_gather | solution.py:604
  221.0 16.0 %shard_map.198 = (bf16[640,1024]{1,0:T(8,128)(2,1)S(1)}, bf16[640,1024]{1,0:T(8,128)(2,1)S(1)}, bf16[640,1024]{1,0:T(8,128)(2,1)S(1)}) custom-call(bf16[640,2560]{1,0:T(8,128)(2,1)} %pad_maximum_fusion.1.x_ref, bf16[640,2560]{1,0:T(8,128)(2,1)} %copy-done.2, bf16[2560,3072]{1,0:T(8,128)(2,1)} %all-gather.5.cloned.1.call-done.gate_ref.up_ref.down_ref.refs_2_.refs_3_.refs_1_, ...), custom_call_target="tpu_custom_call" | custom-call | tf_op jit(solution)/shard_map/pallas_call | solution.py:307
  237.1 10.1 %shard_map.200 = (bf16[320,2560]{1,0:T(8,128)(2,1)S(1)}, bf16[320,2560]{1,0:T(8,128)(2,1)S(1)}) custom-call(bf16[640,1024]{1,0:T(8,128)(2,1)S(1)} %get-tuple-element.36.refs_0_.gate_ref, bf16[640,1024]{1,0:T(8,128)(2,1)S(1)} %get-tuple-element.37.refs_1_.up_ref, ...), custom_call_target="tpu_custom_call" | custom-call | tf_op jit(solution)/shard_map/pallas_call | solution.py:96
  256.5 11.8 %shard_map.215.rest_0_ = bf16[2560,3072]{1,0:T(8,128)(2,1)} custom-call(bf16[640,2560]{1,0:T(8,128)(2,1)} %pad_maximum_fusion.1.x_ref, bf16[640,1024]{1,0:T(8,128)(2,1)S(1)} %get-tuple-element.36.refs_0_.gate_ref, bf16[640,1024]{1,0:T(8,128)(2,1)S(1)} %get-tuple-element.37.refs_1_.up_ref, bf16[4,80,2560]{2,1,0:T(8,128)(2,1)S(1)} %bitcast.177), custom_call_target="tpu_custom_call" | custom-call | tf_op jit(solution)/shard_map/pallas_call | solution.py:251
  268.2 5.1 %collective-permute-done.26.rest_4_ = bf16[80,2560]{1,0:T(8,128)(2,1)S(1)} collective-permute-done((bf16[80,2560]{1,0:T(8,128)(2,1)S(1)}, bf16[80,2560]{1,0:T(8,128)(2,1)S(1)}, u32[]{:S(2)}, u32[]{:S(2)}) %collective-permute-start.26) | collective-permute-done | bytes 409632 | tf_op jit(solution)/shard_map/ppermute | solution.py:28
  273.7 6.3 %shard_map.216 = bf16[2560,3072]{1,0:T(8,128)(2,1)} custom-call(bf16[640,2560]{1,0:T(8,128)(2,1)S(1)} %copy-done.3, bf16[640,1024]{1,0:T(8,128)(2,1)S(1)} %get-tuple-element.40.refs_0_.hidden_ref, bf16[2560,3072]{1,0:T(8,128)(2,1)} %shard_map.215.rest_0_, bf16[80,2560]{1,0:T(8,128)(2,1)S(1)} %get-tuple-element.61.rest_1_, ...), custom_call_target="tpu_custom_call", output_to_operand_aliasing={{}: (2, {})} | custom-call | tf_op jit(solution)/shard_map/pallas_call | solution.py:269
  286.3 4.1 convolution_convert_fusion
  290.4 6.7 %fusion = (f32[5,160]{1,0:T(8,128)S(1)}, f32[2560,160,5]{0,1,2:T(8,128)S(1)}) fusion(f32[5,160]{1,0:T(8,128)S(1)} %broadcast_select_fusion.7, f32[5,160,2560]{2,1,0:T(8,128)} %copy-done.47, f32[5,160]{1,0:T(8,128)S(1)} %broadcast_select_fusion.8, pred[160,2560]{1,0:T(8,128)(4,1)S(1)} %copy-done.52, bf16[20,5,8,256]{3,2,1,0:T(8,128)(2,1)S(1)} %bitcast.216, ...), kind=kOutput, calls=%fused_computation.2 | convolution fusion | flops 1059470592 | bytes 19834240 | tf_op jit(solution)/shard_map/qhd,kd->hqk/dot_general | solution.py:657
  310.3 6.0 %all-to-all-start.3 = ((bf16[16,160,256]{2,1,0:T(8,128)(2,1)}), bf16[16,160,256]{2,1,0:T(8,128)(2,1)S(1)}, u32[]{:S(2)}, u32[]{:S(2)}) async-start(bf16[16,160,256]{2,1,0:T(8,128)(2,1)} %shard_map.203), calls=%async_computation.3 | async-start | bytes 2621440 | tf_op jit(solution)/shard_map/all_to_all | solution.py:32
  335.4 7.5 %shard_map.207 = (bf16[320,2560]{1,0:T(8,128)(2,1)}, bf16[320,2560]{1,0:T(8,128)(2,1)S(1)}) custom-call(bf16[640,1024]{1,0:T(8,128)(2,1)S(1)} %copy-done.20, bf16[2560,3072]{1,0:T(8,128)(2,1)} %all-gather.5.cloned.1.call-done.gate_ref.up_ref.down_ref.refs_2_.refs_3_.refs_1_, bf16[16,40,1280]{2,1,0:T(8,128)(2,1)S(1)} %shard_map.206.refs_2_.refs_1_), custom_call_target="tpu_custom_call" | custom-call | tf_op jit(solution)/shard_map/pallas_call | solution.py:96
  362.1 7.8 %all-to-all-start.4 = ((bf16[16,40,1280]{2,1,0:T(8,128)(2,1)}), bf16[16,40,1280]{2,1,0:T(8,128)(2,1)S(1)}, u32[]{:S(2)}, u32[]{:S(2)}) async-start(bf16[16,40,1280]{2,1,0:T(8,128)(2,1)} %shard_map.212), calls=%async_computation.4 | async-start | bytes 3276800 | tf_op jit(solution)/shard_map/all_to_all | solution.py:32
  379.2 3.9 shard_map.211.refs_0_
  383.1 8.9 %all-to-all-done.4.refs_1_.refs_8_ = bf16[16,40,1280]{2,1,0:T(8,128)(2,1)S(1)} async-done(((bf16[16,40,1280]{2,1,0:T(8,128)(2,1)}), bf16[16,40,1280]{2,1,0:T(8,128)(2,1)S(1)}, u32[]{:S(2)}, u32[]{:S(2)}) %all-to-all-start.4) | async-done | bytes 1638432 | tf_op jit(solution)/shard_map/all_to_all | solution.py:32
  392.0 6.1 %all-to-all-start.5 = ((bf16[16,160,384]{2,1,0:T(8,128)(2,1)}), bf16[16,160,384]{2,1,0:T(8,128)(2,1)}, u32[]{:S(2)}, u32[]{:S(2)}) async-start(bf16[16,160,384]{2,1,0:T(8,128)(2,1)} %shard_map.213), calls=%async_computation.5 | async-start | bytes 3932160 | tf_op jit(solution)/shard_map/all_to_all | solution.py:32
  410.4 10.5 %collective-permute-done.48.refs_2_ = bf16[80,2560]{1,0:T(8,128)(2,1)S(1)} collective-permute-done((bf16[80,2560]{1,0:T(8,128)(2,1)S(1)}, bf16[80,2560]{1,0:T(8,128)(2,1)S(1)}, u32[]{:S(2)}, u32[]{:S(2)}) %collective-permute-start.48) | collective-permute-done | bytes 409632 | tf_op jit(solution)/shard_map/ppermute | solution.py:28
  423.7 6.5 %reduce-scatter.2.cloned.1.call-done = bf16[160,3072]{1,0:T(8,128)(2,1)} async-done(((bf16[2560,3072]{1,0:T(8,128)(2,1)}), bf16[160,3072]{1,0:T(8,128)(2,1)}) %reduce-scatter.2.cloned.1.call-update) | async-done | bytes 983056 | tf_op jit(solution)/shard_map/reduce_scatter | solution.py:645
  439.4 6.1 %collective-permute-done.41.refs_3_ = bf16[40,384]{1,0:T(8,128)(2,1)S(1)} collective-permute-done((bf16[40,384]{1,0:T(8,128)(2,1)S(1)}, bf16[40,384]{1,0:T(8,128)(2,1)S(1)}, u32[]{:S(2)}, u32[]{:S(2)}) %collective-permute-start.41) | collective-permute-done | bytes 30752 | tf_op jit(solution)/shard_map/ppermute | solution.py:28
  449.5 3.8 shard_map.223
  (346 shorter events, 206.2 us)
Async XLA Ops:
  7.2 144.5 %all-gather.3.cloned.1.call-start = ((), (), s32[]{:S(2)}) async-start(), calls=%async_computation.7 | async-start | bytes 6656000 | tf_op jit(solution)/shard_map/all_gather | solution.py:587
  19.9 36.7 %all-to-all-start = ((bf16[16,4,48,384]{3,2,1,0:T(8,128)(2,1)}), bf16[16,4,48,384]{3,2,1,0:T(8,128)(2,1)S(1)}, u32[]{:S(2)}, u32[]{:S(2)}) async-start(bf16[16,4,48,384]{3,2,1,0:T(8,128)(2,1)} %broadcast_in_dim.94), calls=%async_computation | async-start | bytes 4718592 | tf_op jit(solution)/shard_map/all_to_all | solution.py:32
  27.6 193.4 %all-gather.5.cloned.1.call-start = ((), (), s32[]{:S(2)}) async-start(), calls=%async_computation.8 | async-start | bytes 16711680 | tf_op jit(solution)/shard_map/all_gather | solution.py:604
  33.5 18.4 %collective-permute-start.1 = (bf16[80,2560]{1,0:T(8,128)(2,1)S(1)}, bf16[80,2560]{1,0:T(8,128)(2,1)S(1)}, u32[]{:S(2)}, u32[]{:S(2)}) collective-permute-start(bf16[80,2560]{1,0:T(8,128)(2,1)S(1)} %copy.40.refs_0_), channel_id=1, source_target_pairs={{0,64},{32,96},{64,0},{96,32},{1,65},{33,97},{65,1},{97,33},{2,66}... | collective-permute-start | bytes 1228808 | tf_op jit(solution)/shard_map/ppermute | solution.py:28
  35.3 19.2 %collective-permute-start = (bf16[80,2560]{1,0:T(8,128)(2,1)S(1)}, bf16[80,2560]{1,0:T(8,128)(2,1)S(1)}, u32[]{:S(2)}, u32[]{:S(2)}) collective-permute-start(bf16[80,2560]{1,0:T(8,128)(2,1)S(1)} %copy.40.refs_0_), channel_id=1, source_target_pairs={{0,96},{32,0},{64,32},{96,64},{1,97},{33,1},{65,33},{97,65},{2,98}... | collective-permute-start | bytes 1228808 | tf_op jit(solution)/shard_map/ppermute | solution.py:28
  40.0 23.0 %collective-permute-start.19 = (bf16[40,3072]{1,0:T(8,128)(2,1)}, bf16[40,3072]{1,0:T(8,128)(2,1)S(1)}, u32[]{:S(2)}, u32[]{:S(2)}) collective-permute-start(bf16[40,3072]{1,0:T(8,128)(2,1)} %get-tuple-element.79), channel_id=1, source_target_pairs={{0,96},{32,0},{64,32},{96,64},{1,97},{33,1},{65,33},{97,65},{2,98}... | collective-permute-start | bytes 737288 | tf_op jit(solution)/shard_map/ppermute | solution.py:28
  40.0 23.0 %collective-permute-start.18 = (bf16[40,3072]{1,0:T(8,128)(2,1)}, bf16[40,3072]{1,0:T(8,128)(2,1)}, u32[]{:S(2)}, u32[]{:S(2)}) collective-permute-start(bf16[40,3072]{1,0:T(8,128)(2,1)} %get-tuple-element.80), channel_id=1, source_target_pairs={{0,64},{32,96},{64,0},{96,32},{1,65},{33,97},{65,1},{97,33},{2,66}... | collective-permute-start | bytes 737288 | tf_op jit(solution)/shard_map/ppermute | solution.py:28
  44.4 18.7 %collective-permute-start.17 = (bf16[40,3072]{1,0:T(8,128)(2,1)}, bf16[40,3072]{1,0:T(8,128)(2,1)}, u32[]{:S(2)}, u32[]{:S(2)}) collective-permute-start(bf16[40,3072]{1,0:T(8,128)(2,1)} %get-tuple-element.81), channel_id=1, source_target_pairs={{0,32},{32,64},{64,96},{96,0},{1,33},{33,65},{65,97},{97,1},{2,34}... | collective-permute-start | bytes 737288 | tf_op jit(solution)/shard_map/ppermute | solution.py:28
  105.8 31.8 %all-to-all-start.2 = ((bf16[16,160,256]{2,1,0:T(8,128)(2,1)}), bf16[16,160,256]{2,1,0:T(8,128)(2,1)S(1)}, u32[]{:S(2)}, u32[]{:S(2)}) async-start(bf16[16,160,256]{2,1,0:T(8,128)(2,1)} %broadcast_in_dim.96), calls=%async_computation.2 | async-start | bytes 2621440 | tf_op jit(solution)/shard_map/all_to_all | solution.py:32
  113.2 317.1 %reduce-scatter.2.cloned.1.call-start = ((), (), s32[]{:S(2)}) async-start(), calls=%async_computation.9 | async-start | bytes 16711680 | tf_op jit(solution)/shard_map/reduce_scatter | solution.py:645
  117.3 18.6 %collective-permute-start.8 = (bf16[80,2560]{1,0:T(8,128)(2,1)S(1)}, bf16[80,2560]{1,0:T(8,128)(2,1)S(1)}, u32[]{:S(2)}, u32[]{:S(2)}) collective-permute-start(bf16[80,2560]{1,0:T(8,128)(2,1)S(1)} %shard_map.191.refs_0_), channel_id=1, source_target_pairs={{0,64},{32,96},{64,0},{96,32},{1,65},{33,97},{65,1},{97,33},{2,66}... | collective-permute-start | bytes 1228808 | tf_op jit(solution)/shard_map/ppermute | solution.py:28
  119.0 18.5 %collective-permute-start.7 = (bf16[80,2560]{1,0:T(8,128)(2,1)S(1)}, bf16[80,2560]{1,0:T(8,128)(2,1)S(1)}, u32[]{:S(2)}, u32[]{:S(2)}) collective-permute-start(bf16[80,2560]{1,0:T(8,128)(2,1)S(1)} %shard_map.191.refs_0_), channel_id=1, source_target_pairs={{0,96},{32,0},{64,32},{96,64},{1,97},{33,1},{65,33},{97,65},{2,98}... | collective-permute-start | bytes 1228808 | tf_op jit(solution)/shard_map/ppermute | solution.py:28
  140.2 21.1 %collective-permute-start.12 = (bf16[320,2560]{1,0:T(8,128)(2,1)S(1)}, bf16[320,2560]{1,0:T(8,128)(2,1)}, u32[]{:S(2)}, u32[]{:S(2)}) collective-permute-start(bf16[320,2560]{1,0:T(8,128)(2,1)S(1)} %bitcast.180), channel_id=1, source_target_pairs={{0,1},{1,0},{2,3},{3,2},{4,5},{5,4},{6,7},{7,6},{8,9},{9,8},{10,11... | collective-permute-start | bytes 4915208 | tf_op jit(solution)/shard_map/ppermute | solution.py:28
  166.5 21.3 %collective-permute-start.14 = (bf16[80,2560]{1,0:T(8,128)(2,1)S(1)}, bf16[80,2560]{1,0:T(8,128)(2,1)S(1)}, u32[]{:S(2)}, u32[]{:S(2)}) collective-permute-start(bf16[80,2560]{1,0:T(8,128)(2,1)S(1)} %shard_map.194.refs_0_), channel_id=1, source_target_pairs={{0,64},{32,96},{64,0},{96,32},{1,65},{33,97},{65,1},{97,33},{2,66}... | collective-permute-start | bytes 1228808 | tf_op jit(solution)/shard_map/ppermute | solution.py:28
  169.4 18.5 %collective-permute-start.13 = (bf16[80,2560]{1,0:T(8,128)(2,1)S(1)}, bf16[80,2560]{1,0:T(8,128)(2,1)S(1)}, u32[]{:S(2)}, u32[]{:S(2)}) collective-permute-start(bf16[80,2560]{1,0:T(8,128)(2,1)S(1)} %shard_map.194.refs_0_), channel_id=1, source_target_pairs={{0,96},{32,0},{64,32},{96,64},{1,97},{33,1},{65,33},{97,65},{2,98}... | collective-permute-start | bytes 1228808 | tf_op jit(solution)/shard_map/ppermute | solution.py:28
  188.0 24.3 %collective-permute-start.16 = (bf16[320,2560]{1,0:T(8,128)(2,1)S(1)}, bf16[320,2560]{1,0:T(8,128)(2,1)S(1)}, u32[]{:S(2)}, u32[]{:S(2)}) collective-permute-start(bf16[320,2560]{1,0:T(8,128)(2,1)S(1)} %bitcast.186), channel_id=1, source_target_pairs={{0,1},{1,0},{2,3},{3,2},{4,5},{5,4},{6,7},{7,6},{8,9},{9,8},{10,11... | collective-permute-start | bytes 4915208 | tf_op jit(solution)/shard_map/ppermute | solution.py:28
  189.2 21.8 %collective-permute-start.21 = (bf16[160,1280]{1,0:T(8,128)(2,1)S(1)}, bf16[160,1280]{1,0:T(8,128)(2,1)S(1)}, u32[]{:S(2)}, u32[]{:S(2)}) collective-permute-start(bf16[160,1280]{1,0:T(8,128)(2,1)S(1)} %bitcast.191), channel_id=1, source_target_pairs={{0,64},{32,96},{64,0},{96,32},{1,65},{33,97},{65,1},{97,33},{2,66}... | collective-permute-start | bytes 1228808 | tf_op jit(solution)/shard_map/ppermute | solution.py:28
  192.7 18.3 %collective-permute-start.20 = (bf16[160,1280]{1,0:T(8,128)(2,1)S(1)}, bf16[160,1280]{1,0:T(8,128)(2,1)S(1)}, u32[]{:S(2)}, u32[]{:S(2)}) collective-permute-start(bf16[160,1280]{1,0:T(8,128)(2,1)S(1)} %bitcast.192), channel_id=1, source_target_pairs={{0,96},{32,0},{64,32},{96,64},{1,97},{33,1},{65,33},{97,65},{2,98}... | collective-permute-start | bytes 1228808 | tf_op jit(solution)/shard_map/ppermute | solution.py:28
  252.9 20.4 %collective-permute-start.26 = (bf16[80,2560]{1,0:T(8,128)(2,1)S(1)}, bf16[80,2560]{1,0:T(8,128)(2,1)S(1)}, u32[]{:S(2)}, u32[]{:S(2)}) collective-permute-start(bf16[80,2560]{1,0:T(8,128)(2,1)S(1)} %get-tuple-element.73), channel_id=1, source_target_pairs={{0,64},{32,96},{64,0},{96,32},{1,65},{33,97},{65,1},{97,33},{2,66}... | collective-permute-start | bytes 1228808 | tf_op jit(solution)/shard_map/ppermute | solution.py:28
  255.3 18.0 %collective-permute-start.25 = (bf16[80,2560]{1,0:T(8,128)(2,1)S(1)}, bf16[80,2560]{1,0:T(8,128)(2,1)S(1)}, u32[]{:S(2)}, u32[]{:S(2)}) collective-permute-start(bf16[80,2560]{1,0:T(8,128)(2,1)S(1)} %get-tuple-element.74), channel_id=1, source_target_pairs={{0,96},{32,0},{64,32},{96,64},{1,97},{33,1},{65,33},{97,65},{2,98}... | collective-permute-start | bytes 1228808 | tf_op jit(solution)/shard_map/ppermute | solution.py:28
  310.3 34.9 %all-to-all-start.3 = ((bf16[16,160,256]{2,1,0:T(8,128)(2,1)}), bf16[16,160,256]{2,1,0:T(8,128)(2,1)S(1)}, u32[]{:S(2)}, u32[]{:S(2)}) async-start(bf16[16,160,256]{2,1,0:T(8,128)(2,1)} %shard_map.203), calls=%async_computation.3 | async-start | bytes 2621440 | tf_op jit(solution)/shard_map/all_to_all | solution.py:32
  329.0 20.9 %collective-permute-start.30 = (bf16[160,320]{1,0:T(8,128)(2,1)}, bf16[160,320]{1,0:T(8,128)(2,1)}, u32[]{:S(2)}, u32[]{:S(2)}) collective-permute-start(bf16[160,320]{1,0:T(8,128)(2,1)} %get-tuple-element.83), channel_id=1, source_target_pairs={{0,96},{32,0},{64,32},{96,64},{1,97},{33,1},{65,33},{97,65},{2,98}... | collective-permute-start | bytes 307208 | tf_op jit(solution)/shard_map/ppermute | solution.py:28
  329.3 20.8 %collective-permute-start.29 = (bf16[160,320]{1,0:T(8,128)(2,1)}, bf16[160,320]{1,0:T(8,128)(2,1)}, u32[]{:S(2)}, u32[]{:S(2)}) collective-permute-start(bf16[160,320]{1,0:T(8,128)(2,1)} %get-tuple-element.84), channel_id=1, source_target_pairs={{0,64},{32,96},{64,0},{96,32},{1,65},{33,97},{65,1},{97,33},{2,66}... | collective-permute-start | bytes 307208 | tf_op jit(solution)/shard_map/ppermute | solution.py:28
  330.2 19.9 %collective-permute-start.28 = (bf16[160,320]{1,0:T(8,128)(2,1)}, bf16[160,320]{1,0:T(8,128)(2,1)}, u32[]{:S(2)}, u32[]{:S(2)}) collective-permute-start(bf16[160,320]{1,0:T(8,128)(2,1)} %get-tuple-element.85), channel_id=1, source_target_pairs={{0,32},{32,64},{64,96},{96,0},{1,33},{33,65},{65,97},{97,1},{2,34}... | collective-permute-start | bytes 307208 | tf_op jit(solution)/shard_map/ppermute | solution.py:28
  362.1 29.9 %all-to-all-start.4 = ((bf16[16,40,1280]{2,1,0:T(8,128)(2,1)}), bf16[16,40,1280]{2,1,0:T(8,128)(2,1)S(1)}, u32[]{:S(2)}, u32[]{:S(2)}) async-start(bf16[16,40,1280]{2,1,0:T(8,128)(2,1)} %shard_map.212), calls=%async_computation.4 | async-start | bytes 3276800 | tf_op jit(solution)/shard_map/all_to_all | solution.py:32
  373.6 29.4 %collective-permute-start.53 = (bf16[80,2560]{1,0:T(8,128)(2,1)}, bf16[80,2560]{1,0:T(8,128)(2,1)}, u32[]{:S(2)}, u32[]{:S(2)}) collective-permute-start(bf16[80,2560]{1,0:T(8,128)(2,1)} %get-tuple-element.64), channel_id=1, source_target_pairs={{0,64},{32,96},{64,0},{96,32},{1,65},{33,97},{65,1},{97,33},{2,66}... | collective-permute-start | bytes 1228808 | tf_op jit(solution)/shard_map/ppermute | solution.py:28
  374.4 30.2 %collective-permute-start.52 = (bf16[80,2560]{1,0:T(8,128)(2,1)}, bf16[80,2560]{1,0:T(8,128)(2,1)}, u32[]{:S(2)}, u32[]{:S(2)}) collective-permute-start(bf16[80,2560]{1,0:T(8,128)(2,1)} %get-tuple-element.65), channel_id=1, source_target_pairs={{0,96},{32,0},{64,32},{96,64},{1,97},{33,1},{65,33},{97,65},{2,98}... | collective-permute-start | bytes 1228808 | tf_op jit(solution)/shard_map/ppermute | solution.py:28
  375.1 29.6 %collective-permute-start.51 = (bf16[80,2560]{1,0:T(8,128)(2,1)}, bf16[80,2560]{1,0:T(8,128)(2,1)}, u32[]{:S(2)}, u32[]{:S(2)}) collective-permute-start(bf16[80,2560]{1,0:T(8,128)(2,1)} %get-tuple-element.66), channel_id=1, source_target_pairs={{0,32},{32,64},{64,96},{96,0},{1,33},{33,65},{65,97},{97,1},{2,34}... | collective-permute-start | bytes 1228808 | tf_op jit(solution)/shard_map/ppermute | solution.py:28
  392.0 41.9 %all-to-all-start.5 = ((bf16[16,160,384]{2,1,0:T(8,128)(2,1)}), bf16[16,160,384]{2,1,0:T(8,128)(2,1)}, u32[]{:S(2)}, u32[]{:S(2)}) async-start(bf16[16,160,384]{2,1,0:T(8,128)(2,1)} %shard_map.213), calls=%async_computation.5 | async-start | bytes 3932160 | tf_op jit(solution)/shard_map/all_to_all | solution.py:32
  403.0 17.9 %collective-permute-start.48 = (bf16[80,2560]{1,0:T(8,128)(2,1)S(1)}, bf16[80,2560]{1,0:T(8,128)(2,1)S(1)}, u32[]{:S(2)}, u32[]{:S(2)}) collective-permute-start(bf16[80,2560]{1,0:T(8,128)(2,1)S(1)} %get-tuple-element.69), channel_id=1, source_target_pairs={{0,96},{32,0},{64,32},{96,64},{1,97},{33,1},{65,33},{97,65},{2,98}... | collective-permute-start | bytes 1228808 | tf_op jit(solution)/shard_map/ppermute | solution.py:28
  403.0 18.1 %collective-permute-start.47 = (bf16[80,2560]{1,0:T(8,128)(2,1)S(1)}, bf16[80,2560]{1,0:T(8,128)(2,1)S(1)}, u32[]{:S(2)}, u32[]{:S(2)}) collective-permute-start(bf16[80,2560]{1,0:T(8,128)(2,1)S(1)} %get-tuple-element.70), channel_id=1, source_target_pairs={{0,32},{32,64},{64,96},{96,0},{1,33},{33,65},{65,97},{97,1},{2,34}... | collective-permute-start | bytes 1228808 | tf_op jit(solution)/shard_map/ppermute | solution.py:28
  407.5 28.1 %collective-permute-start.54 = (bf16[80,2560]{1,0:T(8,128)(2,1)S(1)}, bf16[80,2560]{1,0:T(8,128)(2,1)}, u32[]{:S(2)}, u32[]{:S(2)}) collective-permute-start(bf16[80,2560]{1,0:T(8,128)(2,1)S(1)} %shard_map.222.refs_15_), channel_id=1, source_target_pairs={{0,1},{1,0},{2,3},{3,2},{4,5},{5,4},{6,7},{7,6},{8,9},{9,8},{10,11... | collective-permute-start | bytes 1228808 | tf_op jit(solution)/shard_map/ppermute | solution.py:28
  (97 other events, 892.3 us)
Sparse Core Ops, SparseCore 0:
  10.9 97.3 all-gather.2
  110.5 110.5 all-gather.4
  280.2 150.0 reduce-scatter.1

commit v2 on v1

--- a/solution.py
+++ b/solution.py
@@ -600,11 +600,11 @@
     x_other = shift(x_own, T, 1)
     mlp_blocks = pack_mlp(w_gate, w_up, w_down)
     mlp_got = to_owners(mlp_blocks)
-    mlp_block = place(mlp_got, Y, x_own, sign=-1).reshape(160, 3072)
-    w_mlp = lax.all_gather(mlp_block, CONTEXT, axis=0, tiled=True)
 
     normed, projected = project(x_own, x_other, gain_one, w_qkv)
     home = exchange(projected, Y)
+    mlp_block = place(mlp_got, Y, home, sign=-1).reshape(160, 3072)
+    w_mlp = lax.all_gather(mlp_block, CONTEXT, axis=0, tiled=True)
     cosine, sine = angles(turned_index - padding, head_dim)
     queries, kv_own = prepare(home, cosine, sine, query_scale)
     kv_mine = exchange(jnp.broadcast_to(kv_own[None], (16, 160, 256)), CONTEXT).reshape(2560, 256)

time: 476 us -> 481 us (1.011)
  starting transfers between devices: 109 us -> 118 us
  local copies, waits for them, and re-layouts: 47.9 us -> 39.7 us
    ppermute x56, waiting for transfers between devices: 118 us -> 134 us  [shift(): return lax.ppermute(x, axis, [(i, (i + by) % n) for i in range(n)])]
    ppermute x56, starting transfers between devices: 70.5 us -> 83.4 us  [shift(): return lax.ppermute(x, axis, [(i, (i + by) % n) for i in range(n)])]
    all_to_all x6, waiting for transfers between devices: 24.5 us -> 12.2 us  [exchange(): return lax.all_to_all(blocks, axis, 0, 0, tiled=True)]
    unnamed x131 -> x129, local copies, waits for them, and re-layouts: 29.6 us -> 22.2 us
  transfers between devices with their start and end apart: 65 -> 65, of which waited for: 37 -> 37; matrix products, arithmetic and copies ran while one was open for 16% -> 15% of each run, Pallas kernels for 10% -> 10%
where the time goes in v2:
time: 481 us; the launch traced here: 472 us
  waiting for transfers between devices  160 us (33%)
  starting transfers between devices  118 us (25%)
  Pallas kernels  82 us (17%)
  local copies, waits for them, and re-layouts  39.7 us (8%)
  matrix products  28.7 us (6%)
  other arithmetic  27.1 us (6%)
  between operations  16 us (3%)
    ppermute x56, waiting for transfers between devices, shift(): return lax.ppermute(x, axis, [(i, (i + by) % n) for i in range(n)])  134 us
    ppermute x56, starting transfers between devices, shift(): return lax.ppermute(x, axis, [(i, (i + by) % n) for i in range(n)])  83.4 us
    all_to_all x6, starting transfers between devices, exchange(): return lax.all_to_all(blocks, axis, 0, 0, tiled=True)  34.6 us
    unnamed x129, local copies, waits for them, and re-layouts  22.2 us
    pallas_call x3, Pallas kernels, row_products(): pl.pallas_call(functools.partial(rows_kernel, count), grid=(n // rows,),...  20.4 us
    pallas_call x1, Pallas kernels, feed_forward(): pl.pallas_call(feed_forward_kernel, grid=(steps,), out_shape=(part, part,...  16 us
    all_to_all x6, waiting for transfers between devices, exchange(): return lax.all_to_all(blocks, axis, 0, 0, tiled=True)  12.2 us
    pallas_call x1, Pallas kernels, gate_up_grads(): pl.pallas_call(gate_up_grad_kernel, grid=(2560 // rows,), out_shape=jax.S...  11.8 us
  transfers between devices with their start and end apart: 65, of which 37 were waited for; matrix products, arithmetic and copies ran while one was open for 15% of the time, Pallas kernels for 10%

profile of v2, /device:TPU:1, one launch (start us, length us, event | category | flops | bytes accessed | tf_op | source)
XLA Modules:
  0.0 471.9 jit_solution(13679356114864691718)
XLA Ops:
  19.9 7.6 %all-to-all-start = ((bf16[16,4,48,384]{3,2,1,0:T(8,128)(2,1)}), bf16[16,4,48,384]{3,2,1,0:T(8,128)(2,1)S(1)}, u32[]{:S(2)}, u32[]{:S(2)}) async-start(bf16[16,4,48,384]{3,2,1,0:T(8,128)(2,1)} %broadcast_in_dim.94), calls=%async_computation | async-start | bytes 4718592 | tf_op jit(solution)/shard_map/all_to_all | solution.py:32
  35.7 7.4 %collective-permute-done.2.refs_3_ = bf16[80,2560]{1,0:T(8,128)(2,1)S(1)} collective-permute-done((bf16[80,2560]{1,0:T(8,128)(2,1)S(1)}, bf16[80,2560]{1,0:T(8,128)(2,1)S(1)}, u32[]{:S(2)}, u32[]{:S(2)}) %collective-permute-start.2) | collective-permute-done | bytes 409632 | tf_op jit(solution)/shard_map/ppermute | solution.py:28
  43.9 6.9 %collective-permute-done.1.refs_2_ = bf16[80,2560]{1,0:T(8,128)(2,1)S(1)} collective-permute-done((bf16[80,2560]{1,0:T(8,128)(2,1)S(1)}, bf16[80,2560]{1,0:T(8,128)(2,1)S(1)}, u32[]{:S(2)}, u32[]{:S(2)}) %collective-permute-start.1) | collective-permute-done | bytes 409632 | tf_op jit(solution)/shard_map/ppermute | solution.py:28
  61.1 5.4 %collective-permute-start.6 = (bf16[4,80,2560]{2,1,0:T(8,128)(2,1)}, bf16[4,80,2560]{2,1,0:T(8,128)(2,1)}, u32[]{:S(2)}, u32[]{:S(2)}) collective-permute-start(bf16[4,80,2560]{2,1,0:T(8,128)(2,1)} %shard_map.188.own_ref), channel_id=1, source_target_pairs={{0,1},{1,0},{2,3},{3,2},{4,5},{5,4},{6,7},{7,6},{8,9},{9,8},{10,11... | collective-permute-start | bytes 4915208 | tf_op jit(solution)/shard_map/ppermute | solution.py:28
  71.5 6.1 %shard_map.189 = (bf16[2,320,2560]{2,1,0:T(8,128)(2,1)}, bf16[4,160,384]{2,1,0:T(8,128)(2,1)}) custom-call(bf16[4,80,2560]{2,1,0:T(8,128)(2,1)} %shard_map.188.own_ref, bf16[4,80,2560]{2,1,0:T(8,128)(2,1)} %collective-permute-done.6.other_ref, f32[1,2560]{1,0:T(1,128)S(1)} %reshape.297.gain_ref, bf16[2560,384]{1,0:T(8,128)(2,1)S(1)} %bitcast.174), custom_call_target="tpu_custom_call" | custom-call | tf_op jit(solution)/shard_map/pallas_call | solution.py:373
  84.9 16.4 %collective-permute-done.19.refs_3_ = bf16[40,3072]{1,0:T(8,128)(2,1)S(1)} collective-permute-done((bf16[40,3072]{1,0:T(8,128)(2,1)S(1)}, bf16[40,3072]{1,0:T(8,128)(2,1)S(1)}, u32[]{:S(2)}, u32[]{:S(2)}) %collective-permute-start.19) | collective-permute-done | bytes 245792 | tf_op jit(solution)/shard_map/ppermute | solution.py:28
  102.7 4.5 collective-permute-done.17.refs_1_
  118.4 6.5 %collective-permute-start.9 = (bf16[80,2560]{1,0:T(8,128)(2,1)S(1)}, bf16[80,2560]{1,0:T(8,128)(2,1)S(1)}, u32[]{:S(2)}, u32[]{:S(2)}) collective-permute-start(bf16[80,2560]{1,0:T(8,128)(2,1)S(1)} %shard_map.191.refs_0_), channel_id=1, source_target_pairs={{0,32},{32,64},{64,96},{96,0},{1,33},{33,65},{65,97},{97,1},{2,34}... | collective-permute-start | bytes 1228808 | tf_op jit(solution)/shard_map/ppermute | solution.py:28
  127.4 5.2 %collective-permute-done.9.refs_3_ = bf16[80,2560]{1,0:T(8,128)(2,1)S(1)} collective-permute-done((bf16[80,2560]{1,0:T(8,128)(2,1)S(1)}, bf16[80,2560]{1,0:T(8,128)(2,1)S(1)}, u32[]{:S(2)}, u32[]{:S(2)}) %collective-permute-start.9) | collective-permute-done | bytes 409632 | tf_op jit(solution)/shard_map/ppermute | solution.py:28
  132.6 9.6 %collective-permute-done.8.refs_2_ = bf16[80,2560]{1,0:T(8,128)(2,1)S(1)} collective-permute-done((bf16[80,2560]{1,0:T(8,128)(2,1)S(1)}, bf16[80,2560]{1,0:T(8,128)(2,1)S(1)}, u32[]{:S(2)}, u32[]{:S(2)}) %collective-permute-start.8) | collective-permute-done | bytes 409632 | tf_op jit(solution)/shard_map/ppermute | solution.py:28
  158.1 5.3 %fusion.52 = f32[160,2560]{1,0:T(8,128)S(1)} fusion(bf16[160,1280]{1,0:T(8,128)(2,1)} %bitcast.188, bf16[2560,1280]{1,0:T(8,128)(2,1)} %all-gather.3.cloned.1.call-done), kind=kOutput, calls=%fused_computation.137 | convolution fusion | flops 1048576000 | bytes 8601600 | tf_op jit(solution)/shard_map/dot_general | solution.py:344
  171.9 4.1 collective-permute-start.15
  178.4 6.4 %collective-permute-done.15.refs_3_ = bf16[80,2560]{1,0:T(8,128)(2,1)S(1)} collective-permute-done((bf16[80,2560]{1,0:T(8,128)(2,1)S(1)}, bf16[80,2560]{1,0:T(8,128)(2,1)S(1)}, u32[]{:S(2)}, u32[]{:S(2)}) %collective-permute-start.15) | collective-permute-done | bytes 409632 | tf_op jit(solution)/shard_map/ppermute | solution.py:28
  184.7 9.7 %collective-permute-done.14.refs_2_ = bf16[80,2560]{1,0:T(8,128)(2,1)S(1)} collective-permute-done((bf16[80,2560]{1,0:T(8,128)(2,1)S(1)}, bf16[80,2560]{1,0:T(8,128)(2,1)S(1)}, u32[]{:S(2)}, u32[]{:S(2)}) %collective-permute-start.14) | collective-permute-done | bytes 409632 | tf_op jit(solution)/shard_map/ppermute | solution.py:28
  201.5 6.3 %collective-permute-done.22.refs_3_ = bf16[160,1280]{1,0:T(8,128)(2,1)S(1)} collective-permute-done((bf16[160,1280]{1,0:T(8,128)(2,1)S(1)}, bf16[160,1280]{1,0:T(8,128)(2,1)S(1)}, u32[]{:S(2)}, u32[]{:S(2)}) %collective-permute-start.22) | collective-permute-done | bytes 409632 | tf_op jit(solution)/shard_map/ppermute | solution.py:28
  207.8 9.5 %collective-permute-done.21.refs_2_ = bf16[160,1280]{1,0:T(8,128)(2,1)S(1)} collective-permute-done((bf16[160,1280]{1,0:T(8,128)(2,1)S(1)}, bf16[160,1280]{1,0:T(8,128)(2,1)S(1)}, u32[]{:S(2)}, u32[]{:S(2)}) %collective-permute-start.21) | collective-permute-done | bytes 409632 | tf_op jit(solution)/shard_map/ppermute | solution.py:28
  220.5 8.4 %all-gather.5.cloned.1.call-done.gate_ref.up_ref.down_ref.refs_2_.refs_3_.refs_1_ = bf16[2560,3072]{1,0:T(8,128)(2,1)} async-done(((bf16[160,3072]{1,0:T(8,128)(2,1)}), bf16[2560,3072]{1,0:T(8,128)(2,1)}) %all-gather.5.cloned.1.call-update) | async-done | bytes 15728656 | tf_op jit(solution)/shard_map/all_gather | solution.py:607
  229.0 16.0 %shard_map.198 = (bf16[640,1024]{1,0:T(8,128)(2,1)S(1)}, bf16[640,1024]{1,0:T(8,128)(2,1)S(1)}, bf16[640,1024]{1,0:T(8,128)(2,1)S(1)}) custom-call(bf16[640,2560]{1,0:T(8,128)(2,1)} %pad_maximum_fusion.1.x_ref, bf16[640,2560]{1,0:T(8,128)(2,1)} %copy-done.2, bf16[2560,3072]{1,0:T(8,128)(2,1)} %all-gather.5.cloned.1.call-done.gate_ref.up_ref.down_ref.refs_2_.refs_3_.refs_1_, ...), custom_call_target="tpu_custom_call" | custom-call | tf_op jit(solution)/shard_map/pallas_call | solution.py:307
  245.0 10.1 %shard_map.200 = (bf16[320,2560]{1,0:T(8,128)(2,1)S(1)}, bf16[320,2560]{1,0:T(8,128)(2,1)S(1)}) custom-call(bf16[640,1024]{1,0:T(8,128)(2,1)S(1)} %get-tuple-element.36.refs_0_.gate_ref, bf16[640,1024]{1,0:T(8,128)(2,1)S(1)} %get-tuple-element.37.refs_1_.up_ref, ...), custom_call_target="tpu_custom_call" | custom-call | tf_op jit(solution)/shard_map/pallas_call | solution.py:96
  264.4 11.8 %shard_map.215.rest_0_ = bf16[2560,3072]{1,0:T(8,128)(2,1)} custom-call(bf16[640,2560]{1,0:T(8,128)(2,1)} %pad_maximum_fusion.1.x_ref, bf16[640,1024]{1,0:T(8,128)(2,1)S(1)} %get-tuple-element.36.refs_0_.gate_ref, bf16[640,1024]{1,0:T(8,128)(2,1)S(1)} %get-tuple-element.37.refs_1_.up_ref, bf16[4,80,2560]{2,1,0:T(8,128)(2,1)S(1)} %bitcast.177), custom_call_target="tpu_custom_call" | custom-call | tf_op jit(solution)/shard_map/pallas_call | solution.py:251
  276.1 5.1 %collective-permute-done.26.rest_4_ = bf16[80,2560]{1,0:T(8,128)(2,1)S(1)} collective-permute-done((bf16[80,2560]{1,0:T(8,128)(2,1)S(1)}, bf16[80,2560]{1,0:T(8,128)(2,1)S(1)}, u32[]{:S(2)}, u32[]{:S(2)}) %collective-permute-start.26) | collective-permute-done | bytes 409632 | tf_op jit(solution)/shard_map/ppermute | solution.py:28
  281.6 6.4 %shard_map.216 = bf16[2560,3072]{1,0:T(8,128)(2,1)} custom-call(bf16[640,2560]{1,0:T(8,128)(2,1)S(1)} %copy-done.3, bf16[640,1024]{1,0:T(8,128)(2,1)S(1)} %get-tuple-element.40.refs_0_.hidden_ref, bf16[2560,3072]{1,0:T(8,128)(2,1)} %shard_map.215.rest_0_, bf16[80,2560]{1,0:T(8,128)(2,1)S(1)} %get-tuple-element.61.rest_1_, ...), custom_call_target="tpu_custom_call", output_to_operand_aliasing={{}: (2, {})} | custom-call | tf_op jit(solution)/shard_map/pallas_call | solution.py:269
  294.2 4.1 convolution_convert_fusion
  298.3 6.7 %fusion = (f32[5,160]{1,0:T(8,128)S(1)}, f32[2560,160,5]{0,1,2:T(8,128)S(1)}) fusion(f32[5,160]{1,0:T(8,128)S(1)} %broadcast_select_fusion.7, f32[5,160,2560]{2,1,0:T(8,128)} %copy-done.46, f32[5,160]{1,0:T(8,128)S(1)} %broadcast_select_fusion.8, pred[160,2560]{1,0:T(8,128)(4,1)S(1)} %copy-done.51, bf16[20,5,8,256]{3,2,1,0:T(8,128)(2,1)S(1)} %bitcast.215, ...), kind=kOutput, calls=%fused_computation.2 | convolution fusion | flops 1059470592 | bytes 19834240 | tf_op jit(solution)/shard_map/qhd,kd->hqk/dot_general | solution.py:657
  318.3 6.0 %all-to-all-start.3 = ((bf16[16,160,256]{2,1,0:T(8,128)(2,1)}), bf16[16,160,256]{2,1,0:T(8,128)(2,1)S(1)}, u32[]{:S(2)}, u32[]{:S(2)}) async-start(bf16[16,160,256]{2,1,0:T(8,128)(2,1)} %shard_map.203), calls=%async_computation.3 | async-start | bytes 2621440 | tf_op jit(solution)/shard_map/all_to_all | solution.py:32
  343.4 7.5 %shard_map.207 = (bf16[320,2560]{1,0:T(8,128)(2,1)}, bf16[320,2560]{1,0:T(8,128)(2,1)S(1)}) custom-call(bf16[640,1024]{1,0:T(8,128)(2,1)S(1)} %copy-done.18, bf16[2560,3072]{1,0:T(8,128)(2,1)} %all-gather.5.cloned.1.call-done.gate_ref.up_ref.down_ref.refs_2_.refs_3_.refs_1_, bf16[16,40,1280]{2,1,0:T(8,128)(2,1)S(1)} %shard_map.206.refs_2_.refs_1_), custom_call_target="tpu_custom_call" | custom-call | tf_op jit(solution)/shard_map/pallas_call | solution.py:96
  370.1 7.8 %all-to-all-start.4 = ((bf16[16,40,1280]{2,1,0:T(8,128)(2,1)}), bf16[16,40,1280]{2,1,0:T(8,128)(2,1)S(1)}, u32[]{:S(2)}, u32[]{:S(2)}) async-start(bf16[16,40,1280]{2,1,0:T(8,128)(2,1)} %shard_map.212), calls=%async_computation.4 | async-start | bytes 3276800 | tf_op jit(solution)/shard_map/all_to_all | solution.py:32
  391.1 8.9 %all-to-all-done.4.refs_1_.refs_8_ = bf16[16,40,1280]{2,1,0:T(8,128)(2,1)S(1)} async-done(((bf16[16,40,1280]{2,1,0:T(8,128)(2,1)}), bf16[16,40,1280]{2,1,0:T(8,128)(2,1)S(1)}, u32[]{:S(2)}, u32[]{:S(2)}) %all-to-all-start.4) | async-done | bytes 1638432 | tf_op jit(solution)/shard_map/all_to_all | solution.py:32
  400.0 6.0 %all-to-all-start.5 = ((bf16[16,160,384]{2,1,0:T(8,128)(2,1)}), bf16[16,160,384]{2,1,0:T(8,128)(2,1)}, u32[]{:S(2)}, u32[]{:S(2)}) async-start(bf16[16,160,384]{2,1,0:T(8,128)(2,1)} %shard_map.213), calls=%async_computation.5 | async-start | bytes 3932160 | tf_op jit(solution)/shard_map/all_to_all | solution.py:32
  418.1 10.5 %collective-permute-done.48.refs_2_ = bf16[80,2560]{1,0:T(8,128)(2,1)S(1)} collective-permute-done((bf16[80,2560]{1,0:T(8,128)(2,1)S(1)}, bf16[80,2560]{1,0:T(8,128)(2,1)S(1)}, u32[]{:S(2)}, u32[]{:S(2)}) %collective-permute-start.48) | collective-permute-done | bytes 409632 | tf_op jit(solution)/shard_map/ppermute | solution.py:28
  431.4 4.7 reduce-scatter.2.cloned.1.call-done
  457.6 4.5 collective-permute-start.55
  (344 shorter events, 214.8 us)
Async XLA Ops:
  7.2 150.9 %all-gather.3.cloned.1.call-start = ((), (), s32[]{:S(2)}) async-start(), calls=%async_computation.7 | async-start | bytes 6656000 | tf_op jit(solution)/shard_map/all_gather | solution.py:587
  19.9 36.6 %all-to-all-start = ((bf16[16,4,48,384]{3,2,1,0:T(8,128)(2,1)}), bf16[16,4,48,384]{3,2,1,0:T(8,128)(2,1)S(1)}, u32[]{:S(2)}, u32[]{:S(2)}) async-start(bf16[16,4,48,384]{3,2,1,0:T(8,128)(2,1)} %broadcast_in_dim.94), calls=%async_computation | async-start | bytes 4718592 | tf_op jit(solution)/shard_map/all_to_all | solution.py:32
  32.2 18.5 %collective-permute-start.1 = (bf16[80,2560]{1,0:T(8,128)(2,1)S(1)}, bf16[80,2560]{1,0:T(8,128)(2,1)S(1)}, u32[]{:S(2)}, u32[]{:S(2)}) collective-permute-start(bf16[80,2560]{1,0:T(8,128)(2,1)S(1)} %copy.40.refs_0_), channel_id=1, source_target_pairs={{0,64},{32,96},{64,0},{96,32},{1,65},{33,97},{65,1},{97,33},{2,66}... | collective-permute-start | bytes 1228808 | tf_op jit(solution)/shard_map/ppermute | solution.py:28
  34.0 19.4 %collective-permute-start = (bf16[80,2560]{1,0:T(8,128)(2,1)S(1)}, bf16[80,2560]{1,0:T(8,128)(2,1)S(1)}, u32[]{:S(2)}, u32[]{:S(2)}) collective-permute-start(bf16[80,2560]{1,0:T(8,128)(2,1)S(1)} %copy.40.refs_0_), channel_id=1, source_target_pairs={{0,96},{32,0},{64,32},{96,64},{1,97},{33,1},{65,33},{97,65},{2,98}... | collective-permute-start | bytes 1228808 | tf_op jit(solution)/shard_map/ppermute | solution.py:28
  77.5 29.7 %all-to-all-start.1 = ((bf16[4,160,384]{2,1,0:T(8,128)(2,1)}), bf16[4,160,384]{2,1,0:T(8,128)(2,1)S(1)}, u32[]{:S(2)}, u32[]{:S(2)}) async-start(bf16[4,160,384]{2,1,0:T(8,128)(2,1)} %get-tuple-element.33), calls=%async_computation.1 | async-start | bytes 983040 | tf_op jit(solution)/shard_map/all_to_all | solution.py:32
  81.0 148.0 %all-gather.5.cloned.1.call-start = ((), (), s32[]{:S(2)}) async-start(), calls=%async_computation.8 | async-start | bytes 16711680 | tf_op jit(solution)/shard_map/all_gather | solution.py:607
  81.1 20.2 %collective-permute-start.19 = (bf16[40,3072]{1,0:T(8,128)(2,1)S(1)}, bf16[40,3072]{1,0:T(8,128)(2,1)S(1)}, u32[]{:S(2)}, u32[]{:S(2)}) collective-permute-start(bf16[40,3072]{1,0:T(8,128)(2,1)S(1)} %get-tuple-element.79), channel_id=1, source_target_pairs={{0,96},{32,0},{64,32},{96,64},{1,97},{33,1},{65,33},{97,65},{2,98}... | collective-permute-start | bytes 737288 | tf_op jit(solution)/shard_map/ppermute | solution.py:28
  83.8 19.0 %collective-permute-start.18 = (bf16[40,3072]{1,0:T(8,128)(2,1)S(1)}, bf16[40,3072]{1,0:T(8,128)(2,1)S(1)}, u32[]{:S(2)}, u32[]{:S(2)}) collective-permute-start(bf16[40,3072]{1,0:T(8,128)(2,1)S(1)} %get-tuple-element.80), channel_id=1, source_target_pairs={{0,64},{32,96},{64,0},{96,32},{1,65},{33,97},{65,1},{97,33},{2,66}... | collective-permute-start | bytes 737288 | tf_op jit(solution)/shard_map/ppermute | solution.py:28
  84.4 22.8 %collective-permute-start.17 = (bf16[40,3072]{1,0:T(8,128)(2,1)S(1)}, bf16[40,3072]{1,0:T(8,128)(2,1)S(1)}, u32[]{:S(2)}, u32[]{:S(2)}) collective-permute-start(bf16[40,3072]{1,0:T(8,128)(2,1)S(1)} %get-tuple-element.81), channel_id=1, source_target_pairs={{0,32},{32,64},{64,96},{96,0},{1,33},{33,65},{65,97},{97,1},{2,34}... | collective-permute-start | bytes 737288 | tf_op jit(solution)/shard_map/ppermute | solution.py:28
  111.9 32.0 %all-to-all-start.2 = ((bf16[16,160,256]{2,1,0:T(8,128)(2,1)}), bf16[16,160,256]{2,1,0:T(8,128)(2,1)S(1)}, u32[]{:S(2)}, u32[]{:S(2)}) async-start(bf16[16,160,256]{2,1,0:T(8,128)(2,1)} %broadcast_in_dim.96), calls=%async_computation.2 | async-start | bytes 2621440 | tf_op jit(solution)/shard_map/all_to_all | solution.py:32
  115.6 320.4 %reduce-scatter.2.cloned.1.call-start = ((), (), s32[]{:S(2)}) async-start(), calls=%async_computation.9 | async-start | bytes 16711680 | tf_op jit(solution)/shard_map/reduce_scatter | solution.py:645
  124.9 17.2 %collective-permute-start.8 = (bf16[80,2560]{1,0:T(8,128)(2,1)S(1)}, bf16[80,2560]{1,0:T(8,128)(2,1)S(1)}, u32[]{:S(2)}, u32[]{:S(2)}) collective-permute-start(bf16[80,2560]{1,0:T(8,128)(2,1)S(1)} %shard_map.191.refs_0_), channel_id=1, source_target_pairs={{0,64},{32,96},{64,0},{96,32},{1,65},{33,97},{65,1},{97,33},{2,66}... | collective-permute-start | bytes 1228808 | tf_op jit(solution)/shard_map/ppermute | solution.py:28
  146.6 20.2 %collective-permute-start.12 = (bf16[320,2560]{1,0:T(8,128)(2,1)S(1)}, bf16[320,2560]{1,0:T(8,128)(2,1)}, u32[]{:S(2)}, u32[]{:S(2)}) collective-permute-start(bf16[320,2560]{1,0:T(8,128)(2,1)S(1)} %bitcast.180), channel_id=1, source_target_pairs={{0,1},{1,0},{2,3},{3,2},{4,5},{5,4},{6,7},{7,6},{8,9},{9,8},{10,11... | collective-permute-start | bytes 4915208 | tf_op jit(solution)/shard_map/ppermute | solution.py:28
  176.0 18.4 %collective-permute-start.14 = (bf16[80,2560]{1,0:T(8,128)(2,1)S(1)}, bf16[80,2560]{1,0:T(8,128)(2,1)S(1)}, u32[]{:S(2)}, u32[]{:S(2)}) collective-permute-start(bf16[80,2560]{1,0:T(8,128)(2,1)S(1)} %shard_map.194.refs_0_), channel_id=1, source_target_pairs={{0,64},{32,96},{64,0},{96,32},{1,65},{33,97},{65,1},{97,33},{2,66}... | collective-permute-start | bytes 1228808 | tf_op jit(solution)/shard_map/ppermute | solution.py:28
  176.1 18.6 %collective-permute-start.13 = (bf16[80,2560]{1,0:T(8,128)(2,1)S(1)}, bf16[80,2560]{1,0:T(8,128)(2,1)S(1)}, u32[]{:S(2)}, u32[]{:S(2)}) collective-permute-start(bf16[80,2560]{1,0:T(8,128)(2,1)S(1)} %shard_map.194.refs_0_), channel_id=1, source_target_pairs={{0,96},{32,0},{64,32},{96,64},{1,97},{33,1},{65,33},{97,65},{2,98}... | collective-permute-start | bytes 1228808 | tf_op jit(solution)/shard_map/ppermute | solution.py:28
  194.8 23.9 %collective-permute-start.16 = (bf16[320,2560]{1,0:T(8,128)(2,1)S(1)}, bf16[320,2560]{1,0:T(8,128)(2,1)S(1)}, u32[]{:S(2)}, u32[]{:S(2)}) collective-permute-start(bf16[320,2560]{1,0:T(8,128)(2,1)S(1)} %bitcast.186), channel_id=1, source_target_pairs={{0,1},{1,0},{2,3},{3,2},{4,5},{5,4},{6,7},{7,6},{8,9},{9,8},{10,11... | collective-permute-start | bytes 4915208 | tf_op jit(solution)/shard_map/ppermute | solution.py:28
  198.1 19.3 %collective-permute-start.21 = (bf16[160,1280]{1,0:T(8,128)(2,1)S(1)}, bf16[160,1280]{1,0:T(8,128)(2,1)S(1)}, u32[]{:S(2)}, u32[]{:S(2)}) collective-permute-start(bf16[160,1280]{1,0:T(8,128)(2,1)S(1)} %bitcast.190), channel_id=1, source_target_pairs={{0,64},{32,96},{64,0},{96,32},{1,65},{33,97},{65,1},{97,33},{2,66}... | collective-permute-start | bytes 1228808 | tf_op jit(solution)/shard_map/ppermute | solution.py:28
  199.0 18.3 %collective-permute-start.20 = (bf16[160,1280]{1,0:T(8,128)(2,1)S(1)}, bf16[160,1280]{1,0:T(8,128)(2,1)S(1)}, u32[]{:S(2)}, u32[]{:S(2)}) collective-permute-start(bf16[160,1280]{1,0:T(8,128)(2,1)S(1)} %bitcast.191), channel_id=1, source_target_pairs={{0,96},{32,0},{64,32},{96,64},{1,97},{33,1},{65,33},{97,65},{2,98}... | collective-permute-start | bytes 1228808 | tf_op jit(solution)/shard_map/ppermute | solution.py:28
  260.8 20.4 %collective-permute-start.26 = (bf16[80,2560]{1,0:T(8,128)(2,1)S(1)}, bf16[80,2560]{1,0:T(8,128)(2,1)S(1)}, u32[]{:S(2)}, u32[]{:S(2)}) collective-permute-start(bf16[80,2560]{1,0:T(8,128)(2,1)S(1)} %get-tuple-element.73), channel_id=1, source_target_pairs={{0,64},{32,96},{64,0},{96,32},{1,65},{33,97},{65,1},{97,33},{2,66}... | collective-permute-start | bytes 1228808 | tf_op jit(solution)/shard_map/ppermute | solution.py:28
  263.2 18.0 %collective-permute-start.25 = (bf16[80,2560]{1,0:T(8,128)(2,1)S(1)}, bf16[80,2560]{1,0:T(8,128)(2,1)S(1)}, u32[]{:S(2)}, u32[]{:S(2)}) collective-permute-start(bf16[80,2560]{1,0:T(8,128)(2,1)S(1)} %get-tuple-element.74), channel_id=1, source_target_pairs={{0,96},{32,0},{64,32},{96,64},{1,97},{33,1},{65,33},{97,65},{2,98}... | collective-permute-start | bytes 1228808 | tf_op jit(solution)/shard_map/ppermute | solution.py:28
  318.3 34.7 %all-to-all-start.3 = ((bf16[16,160,256]{2,1,0:T(8,128)(2,1)}), bf16[16,160,256]{2,1,0:T(8,128)(2,1)S(1)}, u32[]{:S(2)}, u32[]{:S(2)}) async-start(bf16[16,160,256]{2,1,0:T(8,128)(2,1)} %shard_map.203), calls=%async_computation.3 | async-start | bytes 2621440 | tf_op jit(solution)/shard_map/all_to_all | solution.py:32
  337.0 20.8 %collective-permute-start.30 = (bf16[160,320]{1,0:T(8,128)(2,1)}, bf16[160,320]{1,0:T(8,128)(2,1)}, u32[]{:S(2)}, u32[]{:S(2)}) collective-permute-start(bf16[160,320]{1,0:T(8,128)(2,1)} %get-tuple-element.83), channel_id=1, source_target_pairs={{0,96},{32,0},{64,32},{96,64},{1,97},{33,1},{65,33},{97,65},{2,98}... | collective-permute-start | bytes 307208 | tf_op jit(solution)/shard_map/ppermute | solution.py:28
  337.3 20.8 %collective-permute-start.29 = (bf16[160,320]{1,0:T(8,128)(2,1)}, bf16[160,320]{1,0:T(8,128)(2,1)}, u32[]{:S(2)}, u32[]{:S(2)}) collective-permute-start(bf16[160,320]{1,0:T(8,128)(2,1)} %get-tuple-element.84), channel_id=1, source_target_pairs={{0,64},{32,96},{64,0},{96,32},{1,65},{33,97},{65,1},{97,33},{2,66}... | collective-permute-start | bytes 307208 | tf_op jit(solution)/shard_map/ppermute | solution.py:28
  338.2 19.9 %collective-permute-start.28 = (bf16[160,320]{1,0:T(8,128)(2,1)}, bf16[160,320]{1,0:T(8,128)(2,1)}, u32[]{:S(2)}, u32[]{:S(2)}) collective-permute-start(bf16[160,320]{1,0:T(8,128)(2,1)} %get-tuple-element.85), channel_id=1, source_target_pairs={{0,32},{32,64},{64,96},{96,0},{1,33},{33,65},{65,97},{97,1},{2,34}... | collective-permute-start | bytes 307208 | tf_op jit(solution)/shard_map/ppermute | solution.py:28
  370.1 29.9 %all-to-all-start.4 = ((bf16[16,40,1280]{2,1,0:T(8,128)(2,1)}), bf16[16,40,1280]{2,1,0:T(8,128)(2,1)S(1)}, u32[]{:S(2)}, u32[]{:S(2)}) async-start(bf16[16,40,1280]{2,1,0:T(8,128)(2,1)} %shard_map.212), calls=%async_computation.4 | async-start | bytes 3276800 | tf_op jit(solution)/shard_map/all_to_all | solution.py:32
  381.5 29.5 %collective-permute-start.53 = (bf16[80,2560]{1,0:T(8,128)(2,1)}, bf16[80,2560]{1,0:T(8,128)(2,1)}, u32[]{:S(2)}, u32[]{:S(2)}) collective-permute-start(bf16[80,2560]{1,0:T(8,128)(2,1)} %get-tuple-element.64), channel_id=1, source_target_pairs={{0,64},{32,96},{64,0},{96,32},{1,65},{33,97},{65,1},{97,33},{2,66}... | collective-permute-start | bytes 1228808 | tf_op jit(solution)/shard_map/ppermute | solution.py:28
  382.4 30.0 %collective-permute-start.52 = (bf16[80,2560]{1,0:T(8,128)(2,1)}, bf16[80,2560]{1,0:T(8,128)(2,1)}, u32[]{:S(2)}, u32[]{:S(2)}) collective-permute-start(bf16[80,2560]{1,0:T(8,128)(2,1)} %get-tuple-element.65), channel_id=1, source_target_pairs={{0,96},{32,0},{64,32},{96,64},{1,97},{33,1},{65,33},{97,65},{2,98}... | collective-permute-start | bytes 1228808 | tf_op jit(solution)/shard_map/ppermute | solution.py:28
  383.1 29.4 %collective-permute-start.51 = (bf16[80,2560]{1,0:T(8,128)(2,1)}, bf16[80,2560]{1,0:T(8,128)(2,1)}, u32[]{:S(2)}, u32[]{:S(2)}) collective-permute-start(bf16[80,2560]{1,0:T(8,128)(2,1)} %get-tuple-element.66), channel_id=1, source_target_pairs={{0,32},{32,64},{64,96},{96,0},{1,33},{33,65},{65,97},{97,1},{2,34}... | collective-permute-start | bytes 1228808 | tf_op jit(solution)/shard_map/ppermute | solution.py:28
  400.0 39.7 %all-to-all-start.5 = ((bf16[16,160,384]{2,1,0:T(8,128)(2,1)}), bf16[16,160,384]{2,1,0:T(8,128)(2,1)}, u32[]{:S(2)}, u32[]{:S(2)}) async-start(bf16[16,160,384]{2,1,0:T(8,128)(2,1)} %shard_map.213), calls=%async_computation.5 | async-start | bytes 3932160 | tf_op jit(solution)/shard_map/all_to_all | solution.py:32
  410.7 17.9 %collective-permute-start.48 = (bf16[80,2560]{1,0:T(8,128)(2,1)S(1)}, bf16[80,2560]{1,0:T(8,128)(2,1)S(1)}, u32[]{:S(2)}, u32[]{:S(2)}) collective-permute-start(bf16[80,2560]{1,0:T(8,128)(2,1)S(1)} %get-tuple-element.69), channel_id=1, source_target_pairs={{0,96},{32,0},{64,32},{96,64},{1,97},{33,1},{65,33},{97,65},{2,98}... | collective-permute-start | bytes 1228808 | tf_op jit(solution)/shard_map/ppermute | solution.py:28
  411.1 17.5 %collective-permute-start.47 = (bf16[80,2560]{1,0:T(8,128)(2,1)S(1)}, bf16[80,2560]{1,0:T(8,128)(2,1)S(1)}, u32[]{:S(2)}, u32[]{:S(2)}) collective-permute-start(bf16[80,2560]{1,0:T(8,128)(2,1)S(1)} %get-tuple-element.70), channel_id=1, source_target_pairs={{0,32},{32,64},{64,96},{96,0},{1,33},{33,65},{65,97},{97,1},{2,34}... | collective-permute-start | bytes 1228808 | tf_op jit(solution)/shard_map/ppermute | solution.py:28
  415.2 26.1 %collective-permute-start.54 = (bf16[80,2560]{1,0:T(8,128)(2,1)S(1)}, bf16[80,2560]{1,0:T(8,128)(2,1)}, u32[]{:S(2)}, u32[]{:S(2)}) collective-permute-start(bf16[80,2560]{1,0:T(8,128)(2,1)S(1)} %shard_map.222.refs_15_), channel_id=1, source_target_pairs={{0,1},{1,0},{2,3},{3,2},{4,5},{5,4},{6,7},{7,6},{8,9},{9,8},{10,11... | collective-permute-start | bytes 1228808 | tf_op jit(solution)/shard_map/ppermute | solution.py:28
  (96 other events, 873.4 us)
Sparse Core Ops, SparseCore 0:
  10.9 107.8 all-gather.2
  121.0 107.9 all-gather.4
  288.1 147.8 reduce-scatter.1
